TPU v7x, 32 devices: a whole 2x2x4 slice. The times are simulated.
32 devices in a mesh: section: 2 (over core), rows: 16 (over z, y, x).
Axes of the slice: x: 2, y: 2, z: 4, core: 2. Of those that a mesh axis runs over, the one named last changes fastest.
Arguments:
- token_states: bfloat16 [2, 64, 288, 768], P('section', 'rows'), may hold values from -6 to 6
- lengths: int32 [2, 64], P('section', 'rows'), may hold values from 50 to 288, as said below
- key_mask: int32 [2, 64, 288], P('section', 'rows'), may hold values 0 or 1
- cotangent: bfloat16 [2, 64, 288, 768], P('section', 'rows'), may hold values from -6 to 6
- attention_in: bfloat16 [2, 768, 2304], P('section'), may hold values from -0.21875 to 0.21875
- attention_bias: bfloat16 [2, 2, 768], P('section'), may hold values from -1.75 to 1.75
- attention_out: bfloat16 [2, 768, 768], P('section'), may hold values from -1.75 to 1.75
- output_bias: bfloat16 [2, 768], P('section'), may hold values from -1.75 to 1.75
- gain_one: bfloat16 [2, 768], P('section'), may hold values from 0.5 to 1.5
- shift_one: bfloat16 [2, 768], P('section'), may hold values from -1.75 to 1.75
- expand_weight: bfloat16 [2, 768, 3072], P('section'), may hold values from -0.21875 to 0.21875
- expand_bias: bfloat16 [2, 3072], P('section'), may hold values from -1.75 to 1.75
- contract_weight: bfloat16 [2, 3072, 768], P('section'), may hold values from -0.109375 to 0.109375
- contract_bias: bfloat16 [2, 768], P('section'), may hold values from -1.75 to 1.75
- gain_two: bfloat16 [2, 768], P('section'), may hold values from 0.5 to 1.5
- shift_two: bfloat16 [2, 768], P('section'), may hold values from -1.75 to 1.75
- projection: bfloat16 [768, 128], replicated, may hold values from -0.21875 to 0.21875
- passage_table: bfloat16 [4096, 128], replicated, may hold values from -1 to 1
- candidates: int32 [64, 8], P('rows'), may hold values from 0 to 4095
Outputs:
- states_out: float32 [2, 64, 288, 768], P('section', 'rows')
- states_grad: float32 [2, 64, 288, 768], P('section', 'rows')
- grad_attention_in: float32 [2, 768, 2304], P('section', None, 'rows')
- grad_attention_bias: float32 [2, 2, 768], P('section', None, 'rows')
- grad_attention_out: float32 [2, 768, 768], P('section', None, 'rows')
- grad_output_bias: float32 [2, 768], P('section', 'rows')
- grad_gain_one: float32 [2, 768], P('section', 'rows')
- grad_shift_one: float32 [2, 768], P('section', 'rows')
- grad_expand_weight: float32 [2, 768, 3072], P('section', None, 'rows')
- grad_expand_bias: float32 [2, 3072], P('section', 'rows')
- grad_contract_weight: float32 [2, 3072, 768], P('section', None, 'rows')
- grad_contract_bias: float32 [2, 768], P('section', 'rows')
- grad_gain_two: float32 [2, 768], P('section', 'rows')
- grad_shift_two: float32 [2, 768], P('section', 'rows')
- grad_projection: float32 [768, 128], replicated
Inputs may be any that keep to these rules, and one draw needn't show every extreme that they name: `lengths`: in every draw, each section has a sequence of length exactly 288 and one of length exactly 50.
All inputs are finite; a program needn't handle non-finite values. No bound on the sum of `key_mask` on one device may be relied on, other than what follows from the above.
Results may differ from a plain program's by a relative error of at most 0.02.
Values may be sent and summed in bfloat16 or wider, within the bound.
No kernel may reach another device: no remote copies, remote signals or barrier semaphores. Data moves between devices by JAX's collectives and lax.ppermute only.
A program may use at most 320 MiB of HBM per device.

v0:
```python
import math

import jax
import jax.numpy as jnp
from jax import lax
from jax.sharding import PartitionSpec as P

HD = 64
TOPK = 8
MB = 2
SEQ_MB = 2


NEGATIVE = -1000000000.0


def from_behind(value, axis, steps):
    count = lax.axis_size(axis)
    leading, last = (max(0, -steps), min(count, count - steps))
    return lax.ppermute(value, axis, [(source, source + steps) for source in range(leading, last)])


def norm_apply(hidden, gain, shift):
    mean_value = jnp.mean(hidden, axis=-1, keepdims=True)
    centered = hidden - mean_value
    variance = jnp.mean(centered * centered, axis=-1, keepdims=True)
    return centered * lax.rsqrt(variance + 1e-12) * gain + shift


def gelu_exact(values):
    return jax.nn.gelu(values, approximate=False)


def weighting(match):
    return TOPK * jax.nn.softmax(match, axis=-1)[:, 0]


def attention_scores(split, valid):
    scale_factor = 1.0 / math.sqrt(HD)
    scores = (
        jnp.einsum(
            "sqhd,skhd->shqk", split[:, :, 0], split[:, :, 1], preferred_element_type=jnp.float32
        )
        * scale_factor
    )
    return jnp.where(valid[:, None, None, :], scores, NEGATIVE)


def layer_forward(weights, inputs, valid):
    (
        attention_in,
        attention_bias,
        attention_out,
        output_bias,
        gain_one,
        shift_one,
        expand_weight,
        expand_bias,
        contract_weight,
        contract_bias,
        gain_two,
        shift_two,
    ) = weights
    sequences = inputs.shape[0]
    length = inputs.shape[1]
    width = inputs.shape[2]
    heads = width // HD
    flat = inputs.reshape(sequences * length, width)
    flat_low = flat.astype(jnp.bfloat16)
    bias_full = jnp.concatenate(
        [attention_bias[0], jnp.zeros_like(attention_bias[0]), attention_bias[1]]
    ).astype(jnp.float32)
    mixed = (
        jnp.dot(flat_low, attention_in, preferred_element_type=jnp.float32) + bias_full
    ).astype(jnp.bfloat16)
    split = mixed.reshape(sequences, length, 3, heads, HD)
    scores = attention_scores(split, valid)
    top = jnp.max(scores, axis=-1, keepdims=True)
    exponent = jnp.exp(scores - top)
    total = jnp.sum(exponent, axis=-1, keepdims=True)
    attention = exponent / total
    log_total = top + jnp.log(total)
    context = jnp.einsum(
        "shqk,skhd->sqhd",
        attention.astype(jnp.bfloat16),
        split[:, :, 2],
        preferred_element_type=jnp.float32,
    ).astype(jnp.bfloat16)
    context = context.reshape(sequences * length, width)
    attended = jnp.dot(
        context, attention_out, preferred_element_type=jnp.float32
    ) + output_bias.astype(jnp.float32)
    residual_one = flat + attended
    first = norm_apply(residual_one, gain_one, shift_one)
    first_low = first.astype(jnp.bfloat16)
    hidden_pre = jnp.dot(
        first_low, expand_weight, preferred_element_type=jnp.float32
    ) + expand_bias.astype(jnp.float32)
    active = gelu_exact(hidden_pre).astype(jnp.bfloat16)
    feed = jnp.dot(
        active, contract_weight, preferred_element_type=jnp.float32
    ) + contract_bias.astype(jnp.float32)
    residual_two = first + feed
    result = norm_apply(residual_two, gain_two, shift_two)
    kept = (
        flat_low,
        split,
        log_total,
        context,
        residual_one,
        first_low,
        hidden_pre,
        active,
        residual_two,
    )
    return (result.reshape(sequences, length, width), kept)


def layer_backward(weights, kept, valid, grad_result):
    (
        attention_in,
        attention_bias,
        attention_out,
        output_bias,
        gain_one,
        shift_one,
        expand_weight,
        expand_bias,
        contract_weight,
        contract_bias,
        gain_two,
        shift_two,
    ) = weights
    (
        flat_low,
        split,
        log_total,
        context,
        residual_one,
        first_low,
        hidden_pre,
        active,
        residual_two,
    ) = kept
    sequences = split.shape[0]
    length = split.shape[1]
    width = flat_low.shape[1]
    heads = width // HD
    scale_factor = 1.0 / math.sqrt(HD)
    grad_flat = grad_result.reshape(sequences * length, width)
    unused, norm_two_back = jax.vjp(norm_apply, residual_two, gain_two, shift_two)
    grad_residual_two, grad_gain_two, grad_shift_two = norm_two_back(grad_flat)
    grad_feed = grad_residual_two.astype(jnp.bfloat16)
    grad_contract_bias = jnp.sum(grad_feed, axis=0, dtype=jnp.float32)
    grad_contract_weight = jnp.einsum(
        "nf,nd->fd", active, grad_feed, preferred_element_type=jnp.float32
    )
    grad_active = jnp.einsum(
        "nd,fd->nf", grad_feed, contract_weight, preferred_element_type=jnp.float32
    )
    unused, gelu_back = jax.vjp(gelu_exact, hidden_pre)
    grad_hidden = gelu_back(grad_active)[0].astype(jnp.bfloat16)
    grad_expand_bias = jnp.sum(grad_hidden, axis=0, dtype=jnp.float32)
    grad_expand_weight = jnp.einsum(
        "nd,nf->df", first_low, grad_hidden, preferred_element_type=jnp.float32
    )
    grad_first = grad_residual_two + jnp.einsum(
        "nf,df->nd", grad_hidden, expand_weight, preferred_element_type=jnp.float32
    )
    unused, norm_one_back = jax.vjp(norm_apply, residual_one, gain_one, shift_one)
    grad_residual_one, grad_gain_one, grad_shift_one = norm_one_back(grad_first)
    grad_attended = grad_residual_one.astype(jnp.bfloat16)
    grad_output_bias = jnp.sum(grad_attended, axis=0, dtype=jnp.float32)
    grad_attention_out = jnp.einsum(
        "nc,nd->cd", context, grad_attended, preferred_element_type=jnp.float32
    )
    grad_context = jnp.einsum(
        "nd,cd->nc", grad_attended, attention_out, preferred_element_type=jnp.float32
    )
    grad_context = grad_context.astype(jnp.bfloat16).reshape(sequences, length, heads, HD)
    scores = attention_scores(split, valid)
    attention = jnp.exp(scores - log_total)
    grad_attention = jnp.einsum(
        "sqhd,skhd->shqk", grad_context, split[:, :, 2], preferred_element_type=jnp.float32
    )
    grad_value = jnp.einsum(
        "shqk,sqhd->skhd",
        attention.astype(jnp.bfloat16),
        grad_context,
        preferred_element_type=jnp.float32,
    )
    grad_scores = attention * (
        grad_attention - jnp.sum(grad_attention * attention, axis=-1, keepdims=True)
    )
    grad_scores_low = grad_scores.astype(jnp.bfloat16)
    grad_query = (
        jnp.einsum(
            "shqk,skhd->sqhd", grad_scores_low, split[:, :, 1], preferred_element_type=jnp.float32
        )
        * scale_factor
    )
    grad_key = (
        jnp.einsum(
            "shqk,sqhd->skhd", grad_scores_low, split[:, :, 0], preferred_element_type=jnp.float32
        )
        * scale_factor
    )
    grad_mixed = jnp.stack([grad_query, grad_key, grad_value], axis=2).astype(jnp.bfloat16)
    grad_mixed = grad_mixed.reshape(sequences * length, 3 * width)
    grad_attention_bias = jnp.stack(
        [
            jnp.sum(grad_mixed[:, :width], axis=0, dtype=jnp.float32),
            jnp.sum(grad_mixed[:, 2 * width :], axis=0, dtype=jnp.float32),
        ]
    )
    grad_attention_in = jnp.einsum(
        "nc,nm->cm", flat_low, grad_mixed, preferred_element_type=jnp.float32
    )
    grad_inputs = grad_residual_one + jnp.einsum(
        "nm,cm->nc", grad_mixed, attention_in, preferred_element_type=jnp.float32
    )
    gradients = (
        grad_attention_in,
        grad_attention_bias,
        grad_attention_out,
        grad_output_bias,
        grad_gain_one,
        grad_shift_one,
        grad_expand_weight,
        grad_expand_bias,
        grad_contract_weight,
        grad_contract_bias,
        grad_gain_two,
        grad_shift_two,
    )
    return (grad_inputs.reshape(sequences, length, width), gradients)


def body(
    token_states,
    lengths,
    key_mask,
    cotangent,
    attention_in,
    attention_bias,
    attention_out,
    output_bias,
    gain_one,
    shift_one,
    expand_weight,
    expand_bias,
    contract_weight,
    contract_bias,
    gain_two,
    shift_two,
    projection,
    passage_table,
    candidates,
):
    section_index = lax.axis_index("section")
    is_first = section_index == 0
    weights = (
        attention_in[0],
        attention_bias[0],
        attention_out[0],
        output_bias[0],
        gain_one[0].astype(jnp.float32),
        shift_one[0].astype(jnp.float32),
        expand_weight[0],
        expand_bias[0],
        contract_weight[0],
        contract_bias[0],
        gain_two[0].astype(jnp.float32),
        shift_two[0].astype(jnp.float32),
    )
    length = token_states.shape[2]
    width = token_states.shape[3]
    group = SEQ_MB
    positions = jnp.arange(length)
    valid_all = (positions[None, :] < lengths[0][:, None]) & (key_mask[0] == 1) | (
        positions[None, :] == 0
    )
    received_summary = jnp.zeros((group, width), jnp.bfloat16)
    received_embedding = jnp.zeros((group, projection.shape[1]), jnp.bfloat16)
    saved = []
    for tick in range(MB + 1):
        start = jnp.clip(tick - section_index, 0, MB - 1) * group
        block = lax.dynamic_slice_in_dim(token_states[0], start, group, 0).astype(jnp.float32)
        block = block.at[:, 0, :].add(received_summary.astype(jnp.float32))
        valid = lax.dynamic_slice_in_dim(valid_all, start, group, 0)
        result, kept = layer_forward(weights, block, valid)
        summary_low = result[:, 0, :].astype(jnp.bfloat16)
        embedding_low = jnp.dot(summary_low, projection, preferred_element_type=jnp.float32).astype(
            jnp.bfloat16
        )
        saved.append((result, kept, valid, summary_low, received_embedding, received_summary))
        if tick < MB:
            received_summary, received_embedding = from_behind(
                (summary_low, embedding_low), "section", 1
            )
    grad_summary_in = jnp.zeros((group, width), jnp.bfloat16)
    grad_embedding_in = jnp.zeros((group, projection.shape[1]), jnp.bfloat16)
    projection_total = jnp.zeros(projection.shape, jnp.float32)
    gradient_total = jax.tree.map(lambda array: jnp.zeros(array.shape, jnp.float32), weights)
    out_blocks = []
    grad_blocks = []
    for tick in range(MB + 1):
        micro_raw = tick - 1 + section_index
        active_tick = (micro_raw >= 0) & (micro_raw <= MB - 1)
        start = jnp.clip(micro_raw, 0, MB - 1) * group
        earlier = saved[max(tick - 1, 0)]
        later = saved[min(tick + 1, MB)]
        result, kept, valid, summary_low, embedding_seen, summary_seen = jax.tree.map(
            lambda left, right: jnp.where(is_first, left, right), earlier, later
        )
        cot_block = lax.dynamic_slice_in_dim(cotangent[0], start, group, 0).astype(jnp.float32)
        id_block = lax.dynamic_slice_in_dim(candidates, start, group, 0)
        retrieved = jnp.take(passage_table, id_block, axis=0)
        match = jnp.einsum(
            "sp,skp->sk", embedding_seen, retrieved, preferred_element_type=jnp.float32
        )
        weight, weight_back = jax.vjp(weighting, match)
        grad_weight = jnp.sum(cot_block * result, axis=(1, 2))
        grad_match = weight_back(grad_weight)[0].astype(jnp.bfloat16)
        grad_embedding_out = jnp.einsum(
            "sk,skp->sp", grad_match, retrieved, preferred_element_type=jnp.float32
        ).astype(jnp.bfloat16)
        grad_summary = jnp.einsum(
            "sp,dp->sd", grad_embedding_in, projection, preferred_element_type=jnp.float32
        ) + grad_summary_in.astype(jnp.float32)
        grad_result = jnp.where(
            is_first, cot_block.at[:, 0, :].add(grad_summary), weight[:, None, None] * cot_block
        )
        grad_inputs, gradients = layer_backward(weights, kept, valid, grad_result)
        gradients = jax.tree.map(lambda array: jnp.where(active_tick, array, 0.0), gradients)
        gradient_total = jax.tree.map(lambda left, right: left + right, gradient_total, gradients)
        summary_used = jnp.where(is_first, summary_low, summary_seen)
        embedding_grad_used = jnp.where(is_first, grad_embedding_in, grad_embedding_out)
        projection_part = jnp.einsum(
            "sd,sp->dp", summary_used, embedding_grad_used, preferred_element_type=jnp.float32
        )
        projection_total = projection_total + jnp.where(active_tick, projection_part, 0.0)
        out_blocks.append(jnp.where(is_first, result, weight[:, None, None] * result))
        grad_blocks.append(grad_inputs)
        if tick < MB:
            grad_summary_in, grad_embedding_in = from_behind(
                (grad_inputs[:, 0, :].astype(jnp.bfloat16), grad_embedding_out), "section", -1
            )
    (
        grad_attention_in,
        grad_attention_bias,
        grad_attention_out,
        grad_output_bias,
        grad_gain_one,
        grad_shift_one,
        grad_expand_weight,
        grad_expand_bias,
        grad_contract_weight,
        grad_contract_bias,
        grad_gain_two,
        grad_shift_two,
    ) = gradient_total
    reduced = (
        lax.psum_scatter(grad_attention_in, "rows", scatter_dimension=1, tiled=True),
        lax.psum_scatter(grad_attention_bias, "rows", scatter_dimension=1, tiled=True),
        lax.psum_scatter(grad_attention_out, "rows", scatter_dimension=1, tiled=True),
        lax.psum_scatter(grad_output_bias, "rows", scatter_dimension=0, tiled=True),
        lax.psum_scatter(grad_gain_one, "rows", scatter_dimension=0, tiled=True),
        lax.psum_scatter(grad_shift_one, "rows", scatter_dimension=0, tiled=True),
        lax.psum_scatter(grad_expand_weight, "rows", scatter_dimension=1, tiled=True),
        lax.psum_scatter(grad_expand_bias, "rows", scatter_dimension=0, tiled=True),
        lax.psum_scatter(grad_contract_weight, "rows", scatter_dimension=1, tiled=True),
        lax.psum_scatter(grad_contract_bias, "rows", scatter_dimension=0, tiled=True),
        lax.psum_scatter(grad_gain_two, "rows", scatter_dimension=0, tiled=True),
        lax.psum_scatter(grad_shift_two, "rows", scatter_dimension=0, tiled=True),
    )
    projection_grad = lax.psum(projection_total, "rows")
    out_parts = []
    grad_parts = []
    for micro_index in range(MB):
        out_parts.append(jnp.where(is_first, out_blocks[micro_index + 1], out_blocks[micro_index]))
        grad_parts.append(
            jnp.where(is_first, grad_blocks[micro_index + 1], grad_blocks[micro_index])
        )
    states_out = jnp.concatenate(out_parts, axis=0)[None]
    states_grad = jnp.concatenate(grad_parts, axis=0)[None]
    return (
        states_out,
        states_grad,
        reduced[0][None],
        reduced[1][None],
        reduced[2][None],
        reduced[3][None],
        reduced[4][None],
        reduced[5][None],
        reduced[6][None],
        reduced[7][None],
        reduced[8][None],
        reduced[9][None],
        reduced[10][None],
        reduced[11][None],
        projection_grad,
    )


def solution(mesh):
    in_specs = (
        P("section", "rows", None, None),
        P("section", "rows"),
        P("section", "rows", None),
        P("section", "rows", None, None),
        P("section", None, None),
        P("section", None, None),
        P("section", None, None),
        P("section", None),
        P("section", None),
        P("section", None),
        P("section", None, None),
        P("section", None),
        P("section", None, None),
        P("section", None),
        P("section", None),
        P("section", None),
        P(),
        P(),
        P("rows", None),
    )
    out_specs = (
        P("section", "rows", None, None),
        P("section", "rows", None, None),
        P("section", None, "rows"),
        P("section", None, "rows"),
        P("section", None, "rows"),
        P("section", "rows"),
        P("section", "rows"),
        P("section", "rows"),
        P("section", None, "rows"),
        P("section", "rows"),
        P("section", None, "rows"),
        P("section", "rows"),
        P("section", "rows"),
        P("section", "rows"),
        P(),
    )
    return jax.shard_map(body, mesh=mesh, in_specs=in_specs, out_specs=out_specs, check_vma=False)
```

profile of v0, /device:TPU:0, one launch (start us, length us, event | category | flops | bytes accessed | tf_op | source)
XLA Modules:
  0.0 1550.9 jit_solution(6344577107626499685)
XLA Ops:
  20.6 9.3 reshape.889
  29.9 10.1 copy.184
  40.0 4.4 fusion
  61.5 21.2 %fusion.8 = (bf16[576,3072]{1,0:T(8,128)(2,1)S(1)}, f32[576,3072]{1,0:T(8,128)}) fusion(f32[3072]{0:T(1024)S(1)} %bitcast.579, bf16[1,768,3072]{2,1,0:T(8,128)(2,1)} %param.43, f32[576,768]{1,0:T(8,128)S(1)} %get-tuple-element.272, f32[768]{0:T(1024)S(1)} %get-tuple-element.305, f32[768]{0:T(1024)S(1)} %get-tuple-element.306, f32[576]{0:T(1024)S(1)} %add_rsqrt_fusion.5, ...), kind=kOutput, calls=%fused_computation.37 | convolution fusion | flops 2836905984 | bytes 17127936 | tf_op jit(solution)/shard_map/dot_general | solution.py:96
  132.4 9.0 reshape.890
  141.4 10.3 copy.195
  151.8 4.5 fusion.1
  172.7 21.4 %fusion.11 = (bf16[576,3072]{1,0:T(8,128)(2,1)S(1)}, f32[576,3072]{1,0:T(8,128)}) fusion(f32[3072]{0:T(1024)S(1)} %bitcast.580, bf16[1,768,3072]{2,1,0:T(8,128)(2,1)} %param.43, f32[576,768]{1,0:T(8,128)S(1)} %get-tuple-element.280, f32[576]{0:T(1024)S(1)} %add_rsqrt_fusion.3, f32[576]{0:T(1024)S(1)} %broadcast_multiply_fusion.9, ...), kind=kOutput, calls=%fused_computation.40 | convolution fusion | flops 2836905984 | bytes 17127936 | tf_op jit(solution)/shard_map/dot_general | solution.py:96
  236.7 9.0 reshape.891
  245.6 10.2 copy.204
  255.8 4.6 fusion.2
  260.6 4.6 broadcast_select_fusion
  284.9 20.7 %fusion.14 = (bf16[576,3072]{1,0:T(8,128)(2,1)S(1)}, f32[576,3072]{1,0:T(8,128)}) fusion(f32[3072]{0:T(1024)S(1)} %bitcast.581, bf16[576,768]{1,0:T(8,128)(2,1)S(1)} %get-tuple-element.244, bf16[1,768,3072]{2,1,0:T(8,128)(2,1)} %param.43), kind=kOutput, calls=%fused_computation.43 | convolution fusion | flops 2834694144 | bytes 16232448 | tf_op jit(solution)/shard_map/dot_general | solution.py:96
  314.1 16.0 %fusion.137 = (f32[2,288,768]{2,0,1:T(2,128)}, f32[2,288,768]{2,0,1:T(2,128)}, f32[2]{0:T(128)}, f32[2]{0:T(128)}, f32[2]{0:T(128)}, /*index=5*/f32[768]{0:T(1024)}, f32[2,288,768]{2,0,1:T(2,128)S(1)}) fusion(pred[]{:T(512)S(6)} %eq.23, f32[2,288,768]{2,1,0:T(8,128)S(1)} %bitcast.557, f32[2]{0:T(128)S(1)} %copy-done.205, f32[2]{0:T(128)S(1)} %copy-done.201, ...), kind=kLoop, calls=%fused_computation.248 | loop fusion | flops 8846586 | bytes 15043633 | tf_op jit(solution)/shard_map/jit(_where)/select_n | solution.py:381
  333.5 22.5 %convert_reduce_fusion.2 = (f32[3072]{0:T(1024)}, bf16[576,3072]{1,0:T(8,128)(2,1)S(1)}) fusion(f32[576,3072]{1,0:T(8,128)} %get-tuple-element.282, f32[576,3072]{1,0:T(8,128)S(1)} %bitcast.617, f32[3072]{0:T(1024)S(1)} %bitcast.582, pred[]{:T(512)S(6)} %eq.23, bf16[576,768]{1,0:T(8,128)(2,1)S(1)} %get-tuple-element.170, bf16[1,3072,768]{2,1,0:T(8,128)(2,1)S(1)} %bitcast.599), kind=kOutput, calls=%fused_computation.64 | convolution fusion | flops 2854155264 | bytes 23322624 | tf_op jit(solution)/shard_map/nd,fd->nf/dot_general | solution.py:158
  380.8 5.6 multiply_reduce_fusion.2
  402.4 5.4 copy.227
  407.8 8.2 convert_element_type.399
  416.0 6.7 fusion.338
  432.4 7.3 fusion.201
  449.5 7.3 fusion.202
  477.7 22.4 %convert_reduce_fusion.1 = (f32[3072]{0:T(1024)}, bf16[576,3072]{1,0:T(8,128)(2,1)S(1)}) fusion(f32[576,3072]{1,0:T(8,128)} %get-tuple-element.290, f32[576,3072]{1,0:T(8,128)S(1)} %bitcast.619, f32[3072]{0:T(1024)S(1)} %bitcast.583, pred[]{:T(512)S(6)} %eq.23, bf16[576,768]{1,0:T(8,128)(2,1)S(1)} %get-tuple-element.172, bf16[1,3072,768]{2,1,0:T(8,128)(2,1)S(1)} %bitcast.601), kind=kOutput, calls=%fused_computation.63 | convolution fusion | flops 2854155264 | bytes 23322624 | tf_op jit(solution)/shard_map/nd,fd->nf/dot_general | solution.py:158
  513.7 4.5 copy.233
  518.2 8.0 fusion.145
  526.3 8.8 multiply_reduce_fusion.1
  545.4 5.4 copy.238
  550.8 7.9 convert_element_type.409
  558.8 7.1 broadcast_select_fusion.12
  578.5 22.7 %convert_reduce_fusion = (f32[3072]{0:T(1024)}, bf16[576,3072]{1,0:T(8,128)(2,1)S(1)}) fusion(f32[576,3072]{1,0:T(8,128)} %get-tuple-element.290, f32[576,3072]{1,0:T(8,128)S(1)} %bitcast.621, f32[3072]{0:T(1024)S(1)} %bitcast.584, pred[]{:T(512)S(6)} %eq.23, bf16[576,768]{1,0:T(8,128)(2,1)S(1)} %get-tuple-element.174, bf16[1,3072,768]{2,1,0:T(8,128)(2,1)S(1)} %bitcast.603), kind=kOutput, calls=%fused_computation.62 | convolution fusion | flops 2854155264 | bytes 23322624 | tf_op jit(solution)/shard_map/nd,fd->nf/dot_general | solution.py:158
  614.8 4.4 copy.246
  619.3 8.0 fusion.148
  627.3 8.8 multiply_reduce_fusion
  646.4 5.4 copy.251
  651.9 8.0 convert_element_type.423
  681.5 5.3 select_add_fusion.2
  687.5 11.1 fusion.218
  698.7 6.8 fusion.216
  705.5 9.5 select_add_fusion.1
  715.3 6.0 fusion.132
  721.3 6.5 fusion.130
  727.8 10.5 select_add_fusion
  750.8 79.6 %all-reduce.10 = (f32[768]{0:T(1024)}, f32[768]{0:T(1024)}, f32[768]{0:T(1024)}, f32[3072]{0:T(1024)}, f32[768]{0:T(1024)}, /*index=5*/f32[768]{0:T(1024)}, f32[768]{0:T(1024)}) all-reduce(f32[768]{0:T(1024)} %select_add_fusion.10, f32[768]{0:T(1024)} %select_add_fusion.9, ...), channel_id=5, replica_groups=mesh['section'=2,'rows'=16] {'rows'}, use_global_device_ids=true, to_apply=%region_67.69.clone | all-reduce | flops 7680 | bytes 61440
  839.3 5.2 add_select_fusion
  847.9 52.7 %all-reduce.13.cloned.1.call-done = f32[768,128]{1,0:T(8,128)} async-done(((f32[768,128]{1,0:T(8,128)}), f32[768,128]{1,0:T(8,128)}) %all-reduce.13.cloned.1.call-update) | async-done | bytes 393232 | tf_op jit(solution)/shard_map/psum | solution.py:377
  900.6 132.1 %reduce-scatter.10.cloned.1.call-done = f32[768,48]{0,1:T(8,128)} async-done(((f32[768,768]{0,1:T(8,128)}), f32[768,48]{0,1:T(8,128)}) %reduce-scatter.10.cloned.1.call-update) | async-done | bytes 147472 | tf_op jit(solution)/shard_map/reduce_scatter | solution.py:366
  1032.7 156.3 %reduce-scatter.8.cloned.1.call-done = f32[768,144]{0,1:T(8,128)} async-done(((f32[768,2304]{0,1:T(8,128)}), f32[768,144]{0,1:T(8,128)}) %reduce-scatter.8.cloned.1.call-update) | async-done | bytes 442384 | tf_op jit(solution)/shard_map/reduce_scatter | solution.py:364
  1189.0 176.8 %reduce-scatter.12.cloned.1.call-done = f32[768,192]{0,1:T(8,128)} async-done(((f32[768,3072]{0,1:T(8,128)}), f32[768,192]{0,1:T(8,128)}) %reduce-scatter.12.cloned.1.call-update) | async-done | bytes 589840 | tf_op jit(solution)/shard_map/reduce_scatter | solution.py:370
  1365.8 176.3 %reduce-scatter.14.cloned.1.call-done = f32[3072,48]{0,1:T(8,128)} async-done(((f32[3072,768]{0,1:T(8,128)}), f32[3072,48]{0,1:T(8,128)}) %reduce-scatter.14.cloned.1.call-update) | async-done | bytes 589840 | tf_op jit(solution)/shard_map/reduce_scatter | solution.py:372
  (811 shorter events, 357.7 us)
Async XLA Ops:
  7.2 839.4 %reduce-scatter.16.cloned.1.call-start = ((), (), s32[]{:S(2)}) async-start(), calls=%async_computation.10 | async-start | bytes 417792
  13.5 69.2 %copy-start.180 = (f32[768]{0:T(1024)}, f32[768]{0:T(1024)S(1)}, u32[]{:S(2)}) copy-start(f32[768]{0:T(1024)S(1)} %convert_reduce_fusion.17) | copy-start | bytes 9220
  14.2 43.5 %copy-start.183 = (f32[768]{0:T(1024)}, f32[768]{0:T(1024)S(1)}, u32[]{:S(2)}) copy-start(f32[768]{0:T(1024)S(1)} %convert_reduce_fusion.20) | copy-start | bytes 9220
  16.1 30.9 %copy-start.105 = (pred[2,288]{1,0:T(4,128)(4,1)}, pred[2,288]{1,0:T(4,128)(4,1)S(1)}, u32[]{:S(2)}) copy-start(pred[2,288]{1,0:T(4,128)(4,1)S(1)} %get-tuple-element.203) | copy-start | bytes 1732
  57.7 25.1 %slice-start.6 = ((s8[4718592]{0:T(1024)(128)(4,1)}), s8[4194304]{0:T(1024)(128)(4,1)S(1)}, s32[]{:S(2)}) async-start(s8[4718592]{0:T(1024)(128)(4,1)} %bitcast.592), calls=%async_computation.17 | async-start | bytes 8388608
  61.0 21.7 %copy-start.42 = (f32[576,768]{1,0:T(8,128)}, f32[576,768]{1,0:T(8,128)S(1)}, u32[]{:S(2)}) copy-start(f32[576,768]{1,0:T(8,128)S(1)} %get-tuple-element.272) | copy-start | bytes 5308420
  61.1 21.7 %copy-start.130 = (f32[576]{0:T(1024)}, f32[576]{0:T(1024)S(1)}, u32[]{:S(2)}) copy-start(f32[576]{0:T(1024)S(1)} %broadcast_multiply_fusion.11) | copy-start | bytes 6916
  61.4 21.3 %copy-start.185 = (f32[576]{0:T(1024)}, f32[576]{0:T(1024)S(1)}, u32[]{:S(2)}) copy-start(f32[576]{0:T(1024)S(1)} %add_rsqrt_fusion.5) | copy-start | bytes 6916
  61.5 244.2 %copy-start.85 = (f32[768]{0:T(1024)}, f32[768]{0:T(1024)S(1)}, u32[]{:S(2)}) copy-start(f32[768]{0:T(1024)S(1)} %get-tuple-element.305) | copy-start | bytes 9220
  61.5 21.3 %slice-start.7 = ((s8[4718592]{0:T(1024)(128)(4,1)}), s8[524288]{0:T(1024)(128)(4,1)S(1)}, s32[]{:S(2)}) async-start(s8[4718592]{0:T(1024)(128)(4,1)} %bitcast.592), calls=%async_computation.18 | async-start | bytes 1048576
  86.4 111.3 %copy-start.93 = (f32[768]{0:T(1024)}, f32[768]{0:T(1024)S(1)}, u32[]{:S(2)}) copy-start(f32[768]{0:T(1024)S(1)} %get-tuple-element.307) | copy-start | bytes 9220
  88.2 33.8 %collective-permute-start = (bf16[2,768]{1,0:T(2,128)(2,1)}, bf16[2,768]{1,0:T(2,128)(2,1)}, u32[]{:S(2)}, u32[]{:S(2)}) collective-permute-start(bf16[2,768]{1,0:T(2,128)(2,1)} %bitcast.535), channel_id=1, source_target_pairs={{0,16},{1,17},{2,18},{3,19},{4,20},{5,21},{6,22},{7,23},{8,24},{9,... | collective-permute-start | bytes 9224 | tf_op jit(solution)/shard_map/ppermute | solution.py:20
  92.4 121.8 %collective-permute-start.3 = (bf16[2,128]{1,0:T(2,128)(2,1)}, bf16[2,128]{1,0:T(2,128)(2,1)}, u32[]{:S(2)}, u32[]{:S(2)}) collective-permute-start(bf16[2,128]{1,0:T(2,128)(2,1)} %convolution_convert_fusion.3), channel_id=1, source_target_pairs={{0,16},{1,17},{2,18},{3,19},{4,20},{5,21},{6,22},{7,23},{8,24},{9,... | collective-permute-start | bytes 1544 | tf_op jit(solution)/shard_map/ppermute | solution.py:20
  169.0 25.2 %slice-start.8 = ((s8[4718592]{0:T(1024)(128)(4,1)}), s8[4194304]{0:T(1024)(128)(4,1)S(1)}, s32[]{:S(2)}) async-start(s8[4718592]{0:T(1024)(128)(4,1)} %bitcast.594), calls=%async_computation.19 | async-start | bytes 8388608
  172.3 21.8 %copy-start.9 = (f32[576,768]{1,0:T(8,128)}, f32[576,768]{1,0:T(8,128)S(1)}, u32[]{:S(2)}) copy-start(f32[576,768]{1,0:T(8,128)S(1)} %get-tuple-element.280) | copy-start | bytes 5308420
  172.3 21.8 %copy-start.95 = (f32[576]{0:T(1024)}, f32[576]{0:T(1024)S(1)}, u32[]{:S(2)}) copy-start(f32[576]{0:T(1024)S(1)} %broadcast_multiply_fusion.9) | copy-start | bytes 6916
  172.7 21.5 %copy-start.107 = (f32[576]{0:T(1024)}, f32[576]{0:T(1024)S(1)}, u32[]{:S(2)}) copy-start(f32[576]{0:T(1024)S(1)} %add_rsqrt_fusion.3) | copy-start | bytes 6916
  172.7 21.5 %copy-start.181 = (f32[768]{0:T(1024)S(1)}, f32[768]{0:T(1024)}, u32[]{:S(2)}) copy-start(f32[768]{0:T(1024)} %copy-done.180) | copy-start | bytes 9220
  172.7 21.5 %slice-start.9 = ((s8[4718592]{0:T(1024)(128)(4,1)}), s8[524288]{0:T(1024)(128)(4,1)S(1)}, s32[]{:S(2)}) async-start(s8[4718592]{0:T(1024)(128)(4,1)} %bitcast.594), calls=%async_computation.20 | async-start | bytes 1048576
  200.8 13.4 collective-permute-start.2
  209.9 16.6 %collective-permute-start.1 = (bf16[2,768]{1,0:T(2,128)(2,1)}, bf16[2,768]{1,0:T(2,128)(2,1)}, u32[]{:S(2)}, u32[]{:S(2)}) collective-permute-start(bf16[2,768]{1,0:T(2,128)(2,1)} %bitcast.534), channel_id=1, source_target_pairs={{0,16},{1,17},{2,18},{3,19},{4,20},{5,21},{6,22},{7,23},{8,24},{9,... | collective-permute-start | bytes 9224 | tf_op jit(solution)/shard_map/ppermute | solution.py:20
  281.5 24.2 %slice-start.10 = ((s8[4718592]{0:T(1024)(128)(4,1)}), s8[4194304]{0:T(1024)(128)(4,1)S(1)}, s32[]{:S(2)}) async-start(s8[4718592]{0:T(1024)(128)(4,1)} %bitcast.596), calls=%async_computation.21 | async-start | bytes 8388608
  284.9 20.8 %slice-start.11 = ((s8[4718592]{0:T(1024)(128)(4,1)}), s8[524288]{0:T(1024)(128)(4,1)S(1)}, s32[]{:S(2)}) async-start(s8[4718592]{0:T(1024)(128)(4,1)} %bitcast.596), calls=%async_computation.22 | async-start | bytes 1048576
  332.0 24.0 %slice-start.18 = ((s8[4718592]{0:T(1024)(128)(4,1)}), s8[4194304]{0:T(1024)(128)(4,1)S(1)}, s32[]{:S(2)}) async-start(s8[4718592]{0:T(1024)(128)(4,1)} %bitcast.604), calls=%async_computation.29 | async-start | bytes 8388608
  333.4 22.6 %copy-start.71 = (bf16[576,768]{1,0:T(8,128)(2,1)}, bf16[576,768]{1,0:T(8,128)(2,1)S(1)}, u32[]{:S(2)}) copy-start(bf16[576,768]{1,0:T(8,128)(2,1)S(1)} %get-tuple-element.170) | copy-start | bytes 2654212
  333.5 22.5 %slice-start.19 = ((s8[4718592]{0:T(1024)(128)(4,1)}), s8[524288]{0:T(1024)(128)(4,1)S(1)}, s32[]{:S(2)}) async-start(s8[4718592]{0:T(1024)(128)(4,1)} %bitcast.604), calls=%async_computation.30 | async-start | bytes 1048576
  426.0 41.8 %collective-permute-start.4 = (bf16[2,128]{1,0:T(2,128)(2,1)}, bf16[2,128]{1,0:T(2,128)(2,1)}, u32[]{:S(2)}, u32[]{:S(2)}) collective-permute-start(bf16[2,128]{1,0:T(2,128)(2,1)} %convert_element_type.391), channel_id=1, source_target_pairs={{16,0},{17,1},{18,2},{19,3},{20,4},{21,5},{22,6},{23,7},{24,8},{25... | collective-permute-start | bytes 1544 | tf_op jit(solution)/shard_map/ppermute | solution.py:20
  428.7 40.8 %collective-permute-start.5 = (bf16[2,768]{1,0:T(2,128)(2,1)}, bf16[2,768]{1,0:T(2,128)(2,1)}, u32[]{:S(2)}, u32[]{:S(2)}) collective-permute-start(bf16[2,768]{1,0:T(2,128)(2,1)} %bitcast.533), channel_id=1, source_target_pairs={{16,0},{17,1},{18,2},{19,3},{20,4},{21,5},{22,6},{23,7},{24,8},{25... | collective-permute-start | bytes 9224 | tf_op jit(solution)/shard_map/ppermute | solution.py:20
  444.6 21.5 %collective-permute-start.6 = (bf16[2,128]{1,0:T(2,128)(2,1)}, bf16[2,128]{1,0:T(2,128)(2,1)}, u32[]{:S(2)}, u32[]{:S(2)}) collective-permute-start(bf16[2,128]{1,0:T(2,128)(2,1)} %convert_element_type.413), channel_id=1, source_target_pairs={{16,0},{17,1},{18,2},{19,3},{20,4},{21,5},{22,6},{23,7},{24,8},{25... | collective-permute-start | bytes 1544 | tf_op jit(solution)/shard_map/ppermute | solution.py:20
  475.3 24.8 %slice-start.20 = ((s8[4718592]{0:T(1024)(128)(4,1)}), s8[4194304]{0:T(1024)(128)(4,1)S(1)}, s32[]{:S(2)}) async-start(s8[4718592]{0:T(1024)(128)(4,1)} %bitcast.606), calls=%async_computation.31 | async-start | bytes 8388608
  476.8 23.4 %copy-start.72 = (bf16[576,768]{1,0:T(8,128)(2,1)}, bf16[576,768]{1,0:T(8,128)(2,1)S(1)}, u32[]{:S(2)}) copy-start(bf16[576,768]{1,0:T(8,128)(2,1)S(1)} %get-tuple-element.172) | copy-start | bytes 2654212
  477.7 22.5 %copy-start.22 = (f32[576,768]{1,0:T(8,128)S(1)}, f32[576,768]{1,0:T(8,128)}, u32[]{:S(2)}) copy-start(f32[576,768]{1,0:T(8,128)} %get-tuple-element.246) | copy-start | bytes 5308420
  477.7 22.5 %copy-start.116 = (f32[576]{0:T(1024)S(1)}, f32[576]{0:T(1024)}, u32[]{:S(2)}) copy-start(f32[576]{0:T(1024)} %copy-done.115) | copy-start | bytes 6916
  477.7 22.5 %copy-start.136 = (f32[576]{0:T(1024)S(1)}, f32[576]{0:T(1024)}, u32[]{:S(2)}) copy-start(f32[576]{0:T(1024)} %fusion.258) | copy-start | bytes 6916
  477.7 22.5 %slice-start.21 = ((s8[4718592]{0:T(1024)(128)(4,1)}), s8[524288]{0:T(1024)(128)(4,1)S(1)}, s32[]{:S(2)}) async-start(s8[4718592]{0:T(1024)(128)(4,1)} %bitcast.606), calls=%async_computation.32 | async-start | bytes 1048576
  566.0 5.2 collective-permute-start.7
  577.0 24.3 %slice-start.22 = ((s8[4718592]{0:T(1024)(128)(4,1)}), s8[4194304]{0:T(1024)(128)(4,1)S(1)}, s32[]{:S(2)}) async-start(s8[4718592]{0:T(1024)(128)(4,1)} %bitcast.608), calls=%async_computation.33 | async-start | bytes 8388608
  578.4 22.8 %copy-start.60 = (bf16[576,768]{1,0:T(8,128)(2,1)}, bf16[576,768]{1,0:T(8,128)(2,1)S(1)}, u32[]{:S(2)}) copy-start(bf16[576,768]{1,0:T(8,128)(2,1)S(1)} %get-tuple-element.174) | copy-start | bytes 2654212
  578.5 22.8 %copy-start.20 = (f32[576,768]{1,0:T(8,128)S(1)}, f32[576,768]{1,0:T(8,128)}, u32[]{:S(2)}) copy-start(f32[576,768]{1,0:T(8,128)} %get-tuple-element.197) | copy-start | bytes 5308420
  578.5 22.8 %copy-start.112 = (f32[576]{0:T(1024)S(1)}, f32[576]{0:T(1024)}, u32[]{:S(2)}) copy-start(f32[576]{0:T(1024)} %copy-done.111) | copy-start | bytes 6916
  578.5 22.8 %copy-start.134 = (f32[576]{0:T(1024)S(1)}, f32[576]{0:T(1024)}, u32[]{:S(2)}) copy-start(f32[576]{0:T(1024)} %fusion.260) | copy-start | bytes 6916
  578.5 22.8 %slice-start.23 = ((s8[4718592]{0:T(1024)(128)(4,1)}), s8[524288]{0:T(1024)(128)(4,1)S(1)}, s32[]{:S(2)}) async-start(s8[4718592]{0:T(1024)(128)(4,1)} %bitcast.608), calls=%async_computation.34 | async-start | bytes 1048576
  663.4 237.2 %all-reduce.13.cloned.1.call-start = ((), (), s32[]{:S(2)}) async-start(), calls=%async_computation.9 | async-start | bytes 786432 | tf_op jit(solution)/shard_map/psum | solution.py:377
  665.7 367.0 %reduce-scatter.10.cloned.1.call-start = ((), (), s32[]{:S(2)}) async-start(), calls=%async_computation.6 | async-start | bytes 2506752 | tf_op jit(solution)/shard_map/reduce_scatter | solution.py:366
  671.4 517.6 %reduce-scatter.8.cloned.1.call-start = ((), (), s32[]{:S(2)}) async-start(), calls=%async_computation.5 | async-start | bytes 7520256 | tf_op jit(solution)/shard_map/reduce_scatter | solution.py:364
  686.8 678.9 %reduce-scatter.12.cloned.1.call-start = ((), (), s32[]{:S(2)}) async-start(), calls=%async_computation.7 | async-start | bytes 10027008 | tf_op jit(solution)/shard_map/reduce_scatter | solution.py:370
  715.0 827.1 %reduce-scatter.14.cloned.1.call-start = ((), (), s32[]{:S(2)}) async-start(), calls=%async_computation.8 | async-start | bytes 10027008 | tf_op jit(solution)/shard_map/reduce_scatter | solution.py:372
  744.7 94.6 %copy-start.133 = (f32[576]{0:T(1024)S(1)}, f32[576]{0:T(1024)}, u32[]{:S(2)}) copy-start(f32[576]{0:T(1024)} %copy-done.132) | copy-start | bytes 6916
  (217 other events, 1109.1 us)
Sparse Core Ops, SparseCore 0:
  663.5 124.0 reduce-scatter.15
  793.6 106.9 all-reduce.12
  906.1 126.5 reduce-scatter.9
  1039.3 149.6 reduce-scatter.7
  1196.0 169.7 reduce-scatter.11
  1371.9 170.1 reduce-scatter.13
where the time goes:
time: 1560 us; the launch traced here: 1550 us
  waiting for transfers between devices  697 us (45%)
  matrix products  393 us (25%)
  local copies, waits for them, and re-layouts  219 us (14%)
  other arithmetic  128 us (8%)
  blocking collectives  79.6 us (5%)
  between operations  18.9 us (1%)
    reduce_scatter x1, waiting for transfers between devices, body(): lax.psum_scatter(grad_expand_weight, 'rows', scatter_dimension=1, tiled=T...  177 us
    reduce_scatter x1, waiting for transfers between devices, body(): lax.psum_scatter(grad_contract_weight, 'rows', scatter_dimension=1, tiled...  176 us
    reduce_scatter x1, waiting for transfers between devices, body(): lax.psum_scatter(grad_attention_in, 'rows', scatter_dimension=1, tiled=True)  156 us
    reduce_scatter x1, waiting for transfers between devices, body(): lax.psum_scatter(grad_attention_out, 'rows', scatter_dimension=1, tiled=T...  132 us
    unnamed x1, blocking collectives  79.6 us
    dot_general x3, matrix products, layer_backward(): jnp.einsum('nd,fd->nf', grad_feed, contract_weight, preferred_element_typ...  67.7 us
    dot_general x3, matrix products, layer_forward(): jnp.dot(first_low, expand_weight, preferred_element_type=jnp.float32)  63.3 us
    reshape x6, local copies, waits for them, and re-layouts, layer_forward(): split = mixed.reshape(sequences, length, 3, heads, HD)  57.9 us
  transfers between devices with their start and end apart: 14, of which 6 were waited for; matrix products, arithmetic and copies ran while one was open for 17% of the time, Pallas kernels for 0%

commit v1 on v0

v1 whole, which is shorter than its diff:
```python
import functools
import math

import jax
import jax.numpy as jnp
from jax import lax
from jax.experimental import pallas as pl
from jax.experimental.pallas import tpu as pltpu
from jax.sharding import PartitionSpec as P

HD = 64
TOPK = 8
NEGATIVE = -1000000000.0
SCALE = 1.0 / math.sqrt(HD)
LANES = 128
ROW_TILE = 16
F32 = jnp.float32
LOW = jnp.bfloat16
NT = (((1,), (1,)), ((), ()))
TN = (((0,), (0,)), ((), ()))
MIB = 1 << 20


def dot(left, right):
    return jnp.dot(left, right, preferred_element_type=F32)


def dot_nt(left, right):
    return lax.dot_general(left, right, NT, preferred_element_type=F32)


def dot_tn(left, right):
    return lax.dot_general(left, right, TN, preferred_element_type=F32)


def params(limit):
    return pltpu.CompilerParams(vmem_limit_bytes=limit * MIB)


def cost(flops, moved):
    return pl.CostEstimate(flops=int(flops), bytes_accessed=int(moved), transcendentals=0)


ANYWHERE = pl.BlockSpec(memory_space=pl.ANY)


def fixed(shape):
    return pl.BlockSpec(shape, lambda *ids: (0,) * len(shape), pipeline_mode=pl.Buffered(1))


def norm_stats(hidden):
    mean = jnp.mean(hidden, axis=-1, keepdims=True)
    centered = hidden - mean
    root = lax.rsqrt(jnp.mean(centered * centered, axis=-1, keepdims=True) + 1e-12)
    return centered * root, root


def norm_back(grad, gain, normal, root):
    scaled = gain * grad
    mean = jnp.mean(scaled, axis=-1, keepdims=True)
    along = jnp.mean(scaled * normal, axis=-1, keepdims=True)
    return root * (scaled - mean - normal * along)


def gelu_both(u):
    phi = 0.5 + 0.5 * lax.erf(u * (1.0 / math.sqrt(2.0)))
    slope = phi + u * (jnp.exp(-0.5 * u * u) * (1.0 / math.sqrt(2.0 * math.pi)))
    return u * phi, slope


def head_rows(width):
    shape = (ROW_TILE, width)
    return lax.broadcasted_iota(jnp.int32, shape, 1) // HD == lax.broadcasted_iota(jnp.int32, shape, 0)


def pick(ref, row, columns=slice(None)):
    block = ref[:, columns]
    rows = lax.broadcasted_iota(jnp.int32, (block.shape[0], 1), 0)
    return jnp.sum(jnp.where(rows == row, block, 0.0), axis=0, keepdims=True)


def put(ref, row, value, columns=slice(None)):
    block = ref[:, columns]
    rows = lax.broadcasted_iota(jnp.int32, (block.shape[0], 1), 0)
    ref[:, columns] = jnp.where(rows == row, value, block)


def project_kernel(x_ref, w_ref, b_ref, o_ref, x0_ref):
    step = pl.program_id(0)
    bias = b_ref[...].astype(F32)
    bias = jnp.where(step == 0, bias[0:1, :], jnp.where(step == 2, bias[1:2, :], 0.0))
    for part in range(x_ref.shape[1]):
        o_ref[part] = (dot(x_ref[0, part], w_ref[...]) + bias).astype(LOW)
        x0_ref[part : part + 1, :] = x_ref[0, part, 0:1, :].astype(F32)


def project(x, weight, bias):
    _, count, length, width = x.shape
    return pl.pallas_call(
        project_kernel,
        grid=(3,),
        out_shape=(
            jax.ShapeDtypeStruct((count, length, 3 * width), LOW),
            jax.ShapeDtypeStruct((count, width), F32),
        ),
        in_specs=[
            fixed((1, count, length, width)),
            pl.BlockSpec((width, width), lambda i: (0, i)),
            fixed((2, width)),
        ],
        out_specs=(pl.BlockSpec((count, length, width), lambda i: (0, 0, i)), fixed((count, width))),
        compiler_params=params(32),
        cost_estimate=cost(6 * count * length * width * width, 14 * MIB),
        name="project_qkv",
    )(x, weight, bias)


def first_rows_kernel(
    mixed_ref, valid_ref, x0_ref, wo_ref, bo_ref, g1_ref, c1_ref, we_ref, be_ref, wc_ref, bc_ref,
    g2_ref, c2_ref, pr_ref, out_ref, ctx_ref, first_ref, acc_ref,
):
    step = pl.program_id(0)
    count = x0_ref.shape[0]
    width = wo_ref.shape[0]
    chunks = pl.num_programs(0) - count

    @pl.when(step < count)
    def _():
        heads = head_rows(width)
        query = mixed_ref[0, 0:1, 0:width].astype(F32) * SCALE
        spread = jnp.where(heads, query, 0.0).astype(LOW)
        scores = dot_nt(spread, mixed_ref[0, :, width : 2 * width])
        scores = jnp.where(valid_ref[0] > 0, scores, NEGATIVE)
        exponent = jnp.exp(scores - jnp.max(scores, axis=-1, keepdims=True))
        chance = (exponent / jnp.sum(exponent, axis=-1, keepdims=True)).astype(LOW)
        context = dot(chance, mixed_ref[0, :, 2 * width :])
        context = jnp.sum(jnp.where(heads, context, 0.0), axis=0, keepdims=True)
        ctx_ref[pl.ds(step, 1), :] = context

    @pl.when(step == count - 1)
    def _():
        hidden = x0_ref[...] + dot(ctx_ref[0:count, :].astype(LOW), wo_ref[...]) + bo_ref[...].astype(F32)
        normal, root = norm_stats(hidden)
        first_ref[...] = normal * g1_ref[...].astype(F32) + c1_ref[...].astype(F32)

    @pl.when(step >= count)
    def _():
        u = dot(first_ref[...].astype(LOW), we_ref[...]) + be_ref[...].astype(F32)
        active, slope = gelu_both(u)
        part = dot(active.astype(LOW), wc_ref[...])

        @pl.when(step == count)
        def _():
            acc_ref[...] = part

        @pl.when(step > count)
        def _():
            acc_ref[...] += part

    @pl.when(step == pl.num_programs(0) - 1)
    def _():
        normal, root = norm_stats(first_ref[...] + acc_ref[...] + bc_ref[...].astype(F32))
        summary = (normal * g2_ref[...].astype(F32) + c2_ref[...].astype(F32)).astype(LOW)
        out_ref[:, 0:width] = summary
        out_ref[:, width:] = dot(summary, pr_ref[...]).astype(LOW)


def first_rows(mixed, valid, x0, weights, projection):
    (_, _, wo, bo, g1, c1, we, be, wc, bc, g2, c2) = weights
    count, length, wide = mixed.shape
    width, hidden = we.shape
    chunk = 768
    chunks = hidden // chunk
    proj = projection.shape[1]

    def seq(i):
        return jnp.minimum(i, count - 1)

    def part(i):
        return jnp.maximum(i - count, 0)

    row = fixed((1, width))
    return pl.pallas_call(
        first_rows_kernel,
        grid=(count + chunks,),
        out_shape=jax.ShapeDtypeStruct((count, width + proj), LOW),
        in_specs=[
            pl.BlockSpec((1, length, wide), lambda i: (seq(i), 0, 0)),
            pl.BlockSpec((1, 1, length), lambda i: (seq(i), 0, 0)),
            fixed((count, width)),
            fixed((width, width)),
            row, row, row,
            pl.BlockSpec((width, chunk), lambda i: (0, part(i))),
            pl.BlockSpec((1, chunk), lambda i: (0, part(i))),
            pl.BlockSpec((chunk, width), lambda i: (part(i), 0)),
            row, row, row,
            fixed((width, proj)),
        ],
        out_specs=fixed((count, width + proj)),
        scratch_shapes=[
            pltpu.VMEM((8, width), F32),
            pltpu.VMEM((count, width), F32),
            pltpu.VMEM((count, width), F32),
        ],
        compiler_params=params(32),
        cost_estimate=cost(40 * MIB, 17 * MIB),
        name="first_rows_forward",
    )(mixed, valid, x0, wo, bo, g1, c1, we, be, wc, bc, g2, c2, projection)


def with_first(block, row):
    rows = lax.broadcasted_iota(jnp.int32, (ROW_TILE, 1), 0)
    top = jnp.where(rows == 0, row, block[0:ROW_TILE].astype(F32)).astype(block.dtype)
    return jnp.concatenate([top, block[ROW_TILE:]], axis=0)


def pair_of(mixed_ref, m0_ref, pair, width, seq):
    found = []
    for which in range(3):
        columns = pl.ds(which * width + pair * LANES, LANES)
        found.append(with_first(mixed_ref[0, :, columns], pick(m0_ref, seq, columns)))
    return found


def attention_forward_kernel(
    mixed_ref, m0_ref, x_ref, x0_ref, valid_ref, wo_ref, bo_ref, g_ref, c_ref,
    p_ref, ctx_ref, first_ref, low_ref, normal_ref, root_ref, xlow_ref, p0_ref, early_ref, n0_ref, r0_ref,
):
    seq = pl.program_id(0)
    length, width = x_ref.shape[2:]
    valid = valid_ref[0] > 0
    lane = lax.broadcasted_iota(jnp.int32, (1, LANES), 1)
    p0_ref[0] = jnp.zeros(p0_ref.shape[1:], LOW)
    for pair in range(width // LANES):
        columns = pl.ds(pair * LANES, LANES)
        query, key, value = pair_of(mixed_ref, m0_ref, pair, width, seq)
        results = []
        for half in range(2):
            mask = jnp.where(lane // HD == half, SCALE, 0.0).astype(LOW)
            scores = dot_nt(query * mask, key)
            scores = jnp.where(valid, scores, NEGATIVE)
            exponent = jnp.exp(scores - jnp.max(scores, axis=-1, keepdims=True))
            total = jnp.sum(exponent, axis=-1, keepdims=True)
            chance = (exponent * (1.0 / total)).astype(LOW)
            p_ref[0, 2 * pair + half] = chance
            p0_ref[0, 2 * pair + half : 2 * pair + half + 1, :] = chance[0:1, :]
            results.append(dot(chance, value))
        ctx_ref[0, :, columns] = jnp.where(lane < HD, results[0], results[1]).astype(LOW)
    rows = lax.broadcasted_iota(jnp.int32, (length, 1), 0)
    inputs = jnp.where(rows == 0, pick(x0_ref, seq), x_ref[0, 0].astype(F32))
    xlow_ref[0] = inputs.astype(LOW)
    hidden = inputs + dot(ctx_ref[0], wo_ref[...]) + bo_ref[...].astype(F32)
    normal, root = norm_stats(hidden)
    first = normal * g_ref[...].astype(F32) + c_ref[...].astype(F32)
    first_ref[0] = first
    low_ref[0] = first.astype(LOW)
    normal_ref[0] = normal.astype(LOW)
    root_ref[0] = jnp.broadcast_to(root, root_ref.shape[1:])
    put(early_ref, seq, first[0:1, :], slice(0, width))
    put(early_ref, seq, ctx_ref[0, 0:1, :].astype(F32), slice(width, 2 * width))
    put(n0_ref, seq, normal[0:1, :])
    put(r0_ref, seq, jnp.broadcast_to(root[0:1, :], (1, LANES)))


def attention_forward(mixed, m0, x, x0, valid, wo, bo, gain, shift):
    count, length, wide = mixed.shape
    width = wide // 3
    heads = width // HD

    def per(*shape):
        return pl.BlockSpec((1,) + shape, lambda i: (i,) + (0,) * len(shape))

    row = fixed((1, width))
    return pl.pallas_call(
        attention_forward_kernel,
        grid=(count,),
        out_shape=(
            jax.ShapeDtypeStruct((count, heads, length, length), LOW),
            jax.ShapeDtypeStruct((count, length, width), LOW),
            jax.ShapeDtypeStruct((count, length, width), F32),
            jax.ShapeDtypeStruct((count, length, width), LOW),
            jax.ShapeDtypeStruct((count, length, width), LOW),
            jax.ShapeDtypeStruct((count, length, LANES), F32),
            jax.ShapeDtypeStruct((count, length, width), LOW),
            jax.ShapeDtypeStruct((count, ROW_TILE, length), LOW),
            jax.ShapeDtypeStruct((count, 2 * width), F32),
            jax.ShapeDtypeStruct((count, width), F32),
            jax.ShapeDtypeStruct((count, LANES), F32),
        ),
        in_specs=[
            per(length, wide),
            fixed((count, wide)),
            pl.BlockSpec((1, 1, length, width), lambda i: (0, i, 0, 0)),
            fixed((count, width)),
            per(1, length),
            fixed((width, width)),
            row, row, row,
        ],
        out_specs=(
            per(heads, length, length),
            per(length, width),
            per(length, width),
            per(length, width),
            per(length, width),
            per(length, LANES),
            per(length, width),
            per(ROW_TILE, length),
            fixed((count, 2 * width)),
            fixed((count, width)),
            fixed((count, LANES)),
        ),
        compiler_params=params(60),
        cost_estimate=cost(12 * 1000**3, 26 * MIB),
        name="attention_forward",
    )(mixed, m0, x, x0, valid, wo, bo, gain, shift)


def turn(into_ref, from_ref):
    wide = from_ref.shape[1]
    tile = 384 if wide % 384 == 0 else LANES
    for column in range(0, wide, tile):
        into_ref[column : column + tile, :] = from_ref[:, column : column + tile].T


def grad_rows(place_ref, half, at_ref, right, out_ref, shards, kept, offset=0):
    span = at_ref.shape[0] // shards
    pitch = out_ref.shape[0] // (shards // 2)
    per = max(1, 384 // span)
    for group in range(0, shards // 2, per):
        pieces = []
        for shard in range(group, group + per):
            start = pl.multiple_of(place_ref[half, shard + kept * (shards // 2)] * span, ROW_TILE)
            pieces.append(at_ref[pl.ds(start, span), :])
        left = pieces[0] if per == 1 else jnp.concatenate(pieces, axis=0)
        result = dot(left, right).astype(LOW)
        for index in range(per):
            at = (group + index) * pitch + offset
            out_ref[at : at + span, :] = result[index * span : (index + 1) * span]


def feed_forward_kernel(
    place_ref, scal_ref, x_ref, we_ref, be_ref, wc_hbm, first_ref, bc_ref, g_ref, c_ref, cot_ref,
    slope_ref, out_ref, zg_ref, fg_ref, sums_ref, wg_ref, z0_ref, r0_ref, a0_ref, s0_ref,
    send0_ref, send1_ref, keep0_ref, keep1_ref,
    act_ref, wc_ref, feed_ref, low_ref, turned_ref, sem,
    *, chunks, tiles, shards,
):
    step = pl.program_id(0)
    length, width = first_ref.shape[1:]
    count = x_ref.shape[0] // length
    chunk = we_ref.shape[1]
    second = chunks + count + 1
    copy = pltpu.make_async_copy(wc_hbm, wc_ref, sem)

    @pl.when(step == 0)
    def _():
        copy.start()

    @pl.when(step < chunks)
    def _():
        u = dot(x_ref[...], we_ref[...]) + be_ref[...].astype(F32)
        active, slope = gelu_both(u)
        active = active.astype(LOW)
        act_ref[:, pl.ds(pl.multiple_of(step * chunk, LANES), chunk)] = active
        slope_ref[...] = slope.astype(LOW)
        for part in range(count):
            a0_ref[part : part + 1, :] = active[part * length : part * length + 1, :].astype(F32)
            s0_ref[part : part + 1, :] = slope[part * length : part * length + 1, :]

    def feed(seq):
        rows = pl.ds(pl.multiple_of(seq * length, ROW_TILE), length)
        feed_ref[lax.rem(seq, 2)] = dot(act_ref[rows, :], wc_ref[...])

    def norm(seq):
        weight = scal_ref[seq]
        keep = scal_ref[count]
        normal, root = norm_stats(first_ref[0] + feed_ref[lax.rem(seq, 2)] + bc_ref[...].astype(F32))
        gain = g_ref[...].astype(F32)
        result = normal * gain + c_ref[...].astype(F32)
        cot = cot_ref[0].astype(F32)
        out_ref[0] = weight * result
        put(wg_ref, seq, jnp.sum(cot * result, axis=0, keepdims=True))
        put(z0_ref, seq, normal[0:1, :])
        put(r0_ref, seq, jnp.broadcast_to(root[0:1, :], (1, LANES)))
        rows = lax.broadcasted_iota(jnp.int32, (length, 1), 0)
        grad = cot * jnp.where(rows == 0, weight * keep, weight)
        z_grad = norm_back(grad, gain, normal, root)
        zg_ref[0] = z_grad
        feed_grad = z_grad.astype(LOW)
        fg_ref[0] = feed_grad
        low_ref[pl.ds(pl.multiple_of(seq * length, ROW_TILE), length), :] = feed_grad
        sums_ref[0:1, :] += jnp.sum(grad * normal, axis=0, keepdims=True)
        sums_ref[1:2, :] += jnp.sum(grad, axis=0, keepdims=True)
        sums_ref[2:3, :] += jnp.sum(feed_grad.astype(F32), axis=0, keepdims=True)

    @pl.when(step == chunks)
    def _():
        copy.wait()
        sums_ref[...] = jnp.zeros(sums_ref.shape, F32)
        feed(0)

    @pl.when((step > chunks) & (step < second - 1))
    def _():
        feed(step - chunks)
        norm(step - chunks - 1)

    @pl.when(step == second - 1)
    def _():
        norm(count - 1)

    @pl.when(step == second)
    def _():
        turn(turned_ref, low_ref)

    def grads(half, send_ref, keep_ref):
        tile = send_ref.shape[1]
        columns = pl.ds(pl.multiple_of((step - second) * tile, LANES), tile)
        right = act_ref[:, columns]
        grad_rows(place_ref, half, turned_ref, right, send_ref, shards, 0)
        grad_rows(place_ref, half, turned_ref, right, keep_ref, shards, 1)

    @pl.when((step >= second) & (step < second + tiles))
    def _():
        grads(0, send0_ref, keep0_ref)

    @pl.when(step >= second + tiles)
    def _():
        grads(1, send1_ref, keep1_ref)


def feed_forward(place, scal, x, first, we, be, wc, bc, gain, shift, cot, shards):
    count, length, width = first.shape
    rows = count * length
    hidden = we.shape[1]
    chunk = 1024
    chunks = hidden // chunk
    tile = 512
    tiles = hidden // 2 // tile
    second = chunks + count + 1

    def part(i):
        return jnp.minimum(i, chunks - 1)

    def seq(i):
        return jnp.clip(i - chunks - 1, 0, count - 1)

    def early(i):
        return (0, jnp.clip(i - second, 0, tiles - 1))

    def late(i):
        return (0, jnp.clip(i - second - tiles, 0, tiles - 1))

    def per(*shape):
        return pl.BlockSpec((1,) + shape, lambda i: (seq(i),) + (0,) * len(shape))

    row = fixed((1, width))
    cut = jax.ShapeDtypeStruct((width // 2, hidden // 2), LOW)
    block = (width // 2, tile)
    return pl.pallas_call(
        functools.partial(feed_forward_kernel, chunks=chunks, tiles=tiles, shards=shards),
        grid=(second + 2 * tiles,),
        out_shape=(
            jax.ShapeDtypeStruct((rows, hidden), LOW),
            jax.ShapeDtypeStruct((count, length, width), F32),
            jax.ShapeDtypeStruct((count, length, width), F32),
            jax.ShapeDtypeStruct((count, length, width), LOW),
            jax.ShapeDtypeStruct((8, width), F32),
            jax.ShapeDtypeStruct((count, width), F32),
            jax.ShapeDtypeStruct((count, width), F32),
            jax.ShapeDtypeStruct((count, LANES), F32),
            jax.ShapeDtypeStruct((count, hidden), F32),
            jax.ShapeDtypeStruct((count, hidden), F32),
            cut, cut, cut, cut,
        ),
        in_specs=[
            pl.BlockSpec(memory_space=pltpu.SMEM),
            pl.BlockSpec(memory_space=pltpu.SMEM),
            fixed((rows, width)),
            pl.BlockSpec((width, chunk), lambda i: (0, part(i))),
            pl.BlockSpec((1, chunk), lambda i: (0, part(i))),
            ANYWHERE,
            per(length, width),
            row, row, row,
            per(length, width),
        ],
        out_specs=(
            pl.BlockSpec((rows, chunk), lambda i: (0, part(i))),
            per(length, width),
            per(length, width),
            per(length, width),
            fixed((8, width)),
            fixed((count, width)),
            fixed((count, width)),
            fixed((count, LANES)),
            pl.BlockSpec((count, chunk), lambda i: (0, part(i))),
            pl.BlockSpec((count, chunk), lambda i: (0, part(i))),
            pl.BlockSpec(block, early),
            pl.BlockSpec(block, late),
            pl.BlockSpec(block, early),
            pl.BlockSpec(block, late),
        ),
        scratch_shapes=[
            pltpu.VMEM((rows, hidden), LOW),
            pltpu.VMEM((hidden, width), LOW),
            pltpu.VMEM((2, length, width), F32),
            pltpu.VMEM((rows, width), LOW),
            pltpu.VMEM((width, rows), LOW),
            pltpu.SemaphoreType.DMA,
        ],
        compiler_params=params(60),
        cost_estimate=cost(25 * 1000**3, 50 * MIB),
        name="feed_forward",
    )(place, scal, x, we, be, wc, first, bc, gain, shift, cot)


def feed_backward_kernel(
    place_ref, fg_ref, slope_ref, wc_ref, we_hbm, zg_ref, normal_ref, root_ref, g_ref, x_ref,
    eb_ref, hgrad_ref, ag_ref, sums_ref, h0_ref,
    es0_ref, es1_ref, ek0_ref, ek1_ref,
    hg_ref, hidden_ref, we_ref, back_ref, sem,
    *, chunks, shards,
):
    step = pl.program_id(0)
    length, width = zg_ref.shape[1:]
    count = fg_ref.shape[0] // length
    chunk = slope_ref.shape[1]
    second = chunks + count + 1
    copy = pltpu.make_async_copy(we_hbm, we_ref, sem)

    @pl.when(step == 0)
    def _():
        copy.start()

    @pl.when(step < chunks)
    def _():
        grad = (dot_nt(fg_ref[...], wc_ref[...]) * slope_ref[...].astype(F32)).astype(LOW)
        at = pl.multiple_of(step * chunk, LANES)
        hg_ref[:, pl.ds(at, chunk)] = grad
        eb_ref[...] = jnp.sum(grad.astype(F32), axis=0, keepdims=True)
        hidden_ref[pl.ds(at, chunk), :] = grad.T

    def feed(seq):
        rows = pl.ds(pl.multiple_of(seq * length, ROW_TILE), length)
        back_ref[lax.rem(seq, 2)] = dot_nt(hg_ref[rows, :], we_ref[...])

    def norm(seq):
        grad = zg_ref[0] + back_ref[lax.rem(seq, 2)]
        normal = normal_ref[0].astype(F32)
        h_grad = norm_back(grad, g_ref[...].astype(F32), normal, root_ref[0, :, 0:1])
        hgrad_ref[0] = h_grad
        put(h0_ref, seq, h_grad[0:1, :])
        attended = h_grad.astype(LOW)
        ag_ref[0] = attended
        sums_ref[0:1, :] += jnp.sum(grad * normal, axis=0, keepdims=True)
        sums_ref[1:2, :] += jnp.sum(grad, axis=0, keepdims=True)
        sums_ref[2:3, :] += jnp.sum(attended.astype(F32), axis=0, keepdims=True)

    @pl.when(step == chunks)
    def _():
        copy.wait()
        sums_ref[...] = jnp.zeros(sums_ref.shape, F32)
        feed(0)

    @pl.when((step > chunks) & (step < second - 1))
    def _():
        feed(step - chunks)
        norm(step - chunks - 1)

    @pl.when(step == second - 1)
    def _():
        norm(count - 1)

    half = width // 2
    for half_index, send_ref, keep_ref in ((0, es0_ref, ek0_ref), (1, es1_ref, ek1_ref)):
        for kept, out_ref in ((0, send_ref), (1, keep_ref)):

            @pl.when(step == second + 2 * half_index + kept)
            def _():
                right = x_ref[:, half_index * half : (half_index + 1) * half]
                grad_rows(place_ref, half_index, hidden_ref, right, out_ref, shards, kept)


def feed_backward(place, fg, slope, wc, we, zg, normal, root, gain, x, shards):
    count, length, width = zg.shape
    rows, hidden = slope.shape
    chunk = 1024
    chunks = hidden // chunk

    def part(i):
        return jnp.minimum(i, chunks - 1)

    def seq(i):
        return jnp.clip(i - chunks - 1, 0, count - 1)

    def per(*shape):
        return pl.BlockSpec((1,) + shape, lambda i: (seq(i),) + (0,) * len(shape))

    cut = jax.ShapeDtypeStruct((hidden // 2, width // 2), LOW)
    return pl.pallas_call(
        functools.partial(feed_backward_kernel, chunks=chunks, shards=shards),
        grid=(chunks + count + 5,),
        out_shape=(
            jax.ShapeDtypeStruct((1, hidden), F32),
            jax.ShapeDtypeStruct((count, length, width), F32),
            jax.ShapeDtypeStruct((count, length, width), LOW),
            jax.ShapeDtypeStruct((8, width), F32),
            jax.ShapeDtypeStruct((count, width), F32),
            cut, cut, cut, cut,
        ),
        in_specs=[
            pl.BlockSpec(memory_space=pltpu.SMEM),
            fixed((rows, width)),
            pl.BlockSpec((rows, chunk), lambda i: (0, part(i))),
            pl.BlockSpec((chunk, width), lambda i: (part(i), 0)),
            ANYWHERE,
            per(length, width),
            per(length, width),
            per(length, LANES),
            fixed((1, width)),
            fixed((rows, width)),
        ],
        out_specs=(
            pl.BlockSpec((1, chunk), lambda i: (0, part(i))),
            per(length, width),
            per(length, width),
            fixed((8, width)),
            fixed((count, width)),
        )
        + (fixed((hidden // 2, width // 2)),) * 4,
        scratch_shapes=[
            pltpu.VMEM((rows, hidden), LOW),
            pltpu.VMEM((hidden, rows), LOW),
            pltpu.VMEM((width, hidden), LOW),
            pltpu.VMEM((2, length, width), F32),
            pltpu.SemaphoreType.DMA,
        ],
        compiler_params=params(60),
        cost_estimate=cost(25 * 1000**3, 50 * MIB),
        name="feed_backward",
    )(place, fg, slope, wc, we, zg, normal, root, gain, x)


def attention_backward_kernel(
    place_ref, ag_ref, wo_ref, p_ref, mixed_ref, m0_ref, x_ref, ctx_ref, *refs, shards
):
    (
        mg_ref, mg0_ref, s0_ref, s1_ref, k0_ref, k1_ref,
        dctx_ref, all_ref, turned_ref, low_ref, other_ref,
    ) = refs[-11:]
    step = pl.program_id(0)
    length, width = ag_ref.shape[1:]
    count = x_ref.shape[0] // length

    @pl.when(step < count)
    def _():
        dctx_ref[...] = dot_nt(ag_ref[0], wo_ref[...]).astype(LOW)
        lane = lax.broadcasted_iota(jnp.int32, (1, LANES), 1)
        rows = pl.ds(pl.multiple_of(step * length, ROW_TILE), length)
        low_ref[rows, :] = ag_ref[0]
        for pair in range(width // LANES):
            query, key, value = pair_of(mixed_ref, m0_ref, pair, width, step)
            grad = dctx_ref[:, pl.ds(pair * LANES, LANES)]
            grads = []
            for half in range(2):
                mask = jnp.where(lane // HD == half, 1.0, 0.0).astype(LOW)
                chance_low = p_ref[0, 2 * pair + half]
                chance = chance_low.astype(F32)
                p_grad = dot_nt(grad * mask, value)
                inner = jnp.sum(p_grad * chance, axis=-1, keepdims=True)
                s_grad = (chance * (p_grad - inner)).astype(LOW)
                grads.append((dot(s_grad, key), dot_tn(s_grad, query), dot_tn(chance_low, grad)))
            for which in range(3):
                both = jnp.where(lane < HD, grads[0][which], grads[1][which])
                if which < 2:
                    both = both * SCALE
                columns = pl.ds(which * width + pair * LANES, LANES)
                low = both.astype(LOW)
                mg_ref[0, :, columns] = low
                all_ref[rows, columns] = low
                put(mg0_ref, step, low[0:1, :].astype(F32), columns)

    @pl.when(step == count)
    def _():
        turn(turned_ref, all_ref)
        turn(other_ref, low_ref)

    half = width // 2
    for half_index, send_ref, keep_ref in ((0, s0_ref, k0_ref), (1, s1_ref, k1_ref)):
        for kept, out_ref in ((0, send_ref), (1, keep_ref)):

            @pl.when(step == count + 2 * half_index + kept)
            def _():
                columns = slice(half_index * half, (half_index + 1) * half)
                grad_rows(place_ref, half_index, turned_ref, x_ref[:, columns], out_ref, shards, kept)
                at = turned_ref.shape[0] // shards
                grad_rows(place_ref, half_index, other_ref, ctx_ref[:, columns], out_ref, shards, kept, at)


def attention_backward(place, ag, wo, p, mixed, m0, x, ctx, after, shards):
    count, length, wide = mixed.shape
    width = wide // 3
    heads = width // HD
    rows = count * length

    def per(*shape):
        return pl.BlockSpec((1,) + shape, lambda i: (jnp.minimum(i, count - 1),) + (0,) * len(shape))

    cut = ((wide + width) // 2, width // 2)
    return pl.pallas_call(
        functools.partial(attention_backward_kernel, shards=shards),
        grid=(count + 4,),
        out_shape=(
            jax.ShapeDtypeStruct((count, length, wide), LOW),
            jax.ShapeDtypeStruct((count, wide), F32),
        )
        + (jax.ShapeDtypeStruct(cut, LOW),) * 4,
        in_specs=[
            pl.BlockSpec(memory_space=pltpu.SMEM),
            per(length, width),
            fixed((width, width)),
            per(heads, length, length),
            per(length, wide),
            fixed((count, wide)),
            fixed((rows, width)),
            fixed((rows, width)),
        ]
        + [ANYWHERE] * len(after),
        out_specs=(per(length, wide), fixed((count, wide))) + (fixed(cut),) * 4,
        scratch_shapes=[
            pltpu.VMEM((length, width), LOW),
            pltpu.VMEM((rows, wide), LOW),
            pltpu.VMEM((wide, rows), LOW),
            pltpu.VMEM((rows, width), LOW),
            pltpu.VMEM((width, rows), LOW),
        ],
        compiler_params=params(60),
        cost_estimate=cost(24 * 1000**3, 32 * MIB),
        name="attention_backward",
    )(place, ag, wo, p, mixed, m0, x, ctx, *after)


def shard_groups(count, wide):
    span = wide // count
    first = [span * shard // HD for shard in range(count)]
    most = max((span * shard + span - 1) // HD - first[shard] + 1 for shard in range(count))
    return [min(one, wide // HD - most) for one in first], most


def input_grad_kernel(mg_ref, w_ref, hgrad_ref, *refs):
    out_ref, sums_ref = refs[-2:]
    width = hgrad_ref.shape[2]
    out_ref[0] = dot_nt(mg_ref[0], w_ref[...]) + hgrad_ref[0]

    @pl.when(pl.program_id(0) == 0)
    def _():
        sums_ref[...] = jnp.zeros(sums_ref.shape, F32)

    sums_ref[0:1, :] += jnp.sum(mg_ref[0, :, 0:width].astype(F32), axis=0, keepdims=True)
    sums_ref[1:2, :] += jnp.sum(mg_ref[0, :, 2 * width :].astype(F32), axis=0, keepdims=True)


def input_grad(mg, weight, hgrad, after):
    count, length, wide = mg.shape
    width = wide // 3

    def per(*shape):
        return pl.BlockSpec((1,) + shape, lambda i: (i,) + (0,) * len(shape))

    return pl.pallas_call(
        input_grad_kernel,
        grid=(count,),
        out_shape=(jax.ShapeDtypeStruct((count, length, width), F32), jax.ShapeDtypeStruct((8, width), F32)),
        in_specs=[per(length, wide), fixed((width, wide)), per(length, width)] + [ANYWHERE] * len(after),
        out_specs=(per(length, width), fixed((8, width))),
        compiler_params=params(40),
        cost_estimate=cost(6 * 1000**3, 16 * MIB),
        name="input_grad",
    )(mg, weight, hgrad, *after)


def last_kernel(
    g0_ref, z0_ref, r2_ref, g2_ref, slope_ref, wc_ref, we_ref, n0_ref, r1_ref, g1_ref, wo_ref, wi_hbm,
    p0_ref, mixed_ref, m0_ref, x_ref, main_ref, s2_ref, s1_ref, s0_ref, eb_ref, *refs, groups
):
    (
        out_ref, hg_ref, fg_ref, ag_ref, coef_ref, y_ref, sums_ref, ebout_ref,
        zg_ref, acc_ref, hz_ref, dctx_ref, rows_ref, wi_ref, sem,
    ) = refs[-15:]
    step = pl.program_id(0)
    count, width = g0_ref.shape
    chunks = pl.num_programs(0) - count
    copy = pltpu.make_async_copy(wi_hbm, wi_ref, sem)

    @pl.when(step == 0)
    def _():
        copy.start()
        grad = g0_ref[...]
        z_grad = norm_back(grad, g2_ref[...].astype(F32), z0_ref[...], r2_ref[:, 0:1])
        zg_ref[...] = z_grad
        low = z_grad.astype(LOW)
        fg_ref[...] = low
        sums_ref[0:2, :] = s0_ref[0:2, :]
        sums_ref[6:7, :] = s2_ref[0:1, :] + jnp.sum(grad * z0_ref[...], axis=0, keepdims=True)
        sums_ref[7:8, :] = s2_ref[1:2, :] + jnp.sum(grad, axis=0, keepdims=True)
        sums_ref[5:6, :] = s2_ref[2:3, :] + jnp.sum(low.astype(F32), axis=0, keepdims=True)
        acc_ref[...] = jnp.zeros(acc_ref.shape, F32)

    @pl.when(step < chunks)
    def _():
        grad = (dot_nt(fg_ref[...], wc_ref[...]) * slope_ref[...].astype(F32)).astype(LOW)
        hg_ref[...] = grad
        ebout_ref[...] = eb_ref[...] + jnp.sum(grad.astype(F32), axis=0, keepdims=True)
        acc_ref[...] += dot_nt(grad, we_ref[...])

    @pl.when(step == chunks - 1)
    def _():
        grad = zg_ref[...] + acc_ref[...]
        normal = n0_ref[...]
        h_grad = norm_back(grad, g1_ref[...].astype(F32), normal, r1_ref[:, 0:1])
        hz_ref[0:count, :] = h_grad
        low = h_grad.astype(LOW)
        ag_ref[...] = low
        sums_ref[3:4, :] = s1_ref[0:1, :] + jnp.sum(grad * normal, axis=0, keepdims=True)
        sums_ref[4:5, :] = s1_ref[1:2, :] + jnp.sum(grad, axis=0, keepdims=True)
        sums_ref[2:3, :] = s1_ref[2:3, :] + jnp.sum(low.astype(F32), axis=0, keepdims=True)
        dctx_ref[0:count, :] = dot_nt(low, wo_ref[...])
        copy.wait()

    @pl.when(step >= chunks)
    def _():
        seq = step - chunks
        heads = head_rows(width)
        own = dctx_ref[pl.ds(seq, 1), :]
        grad = jnp.where(heads, own, 0.0).astype(LOW)
        query0 = pick(m0_ref, seq, slice(0, width))
        query = jnp.where(heads, query0, 0.0).astype(LOW)
        key = with_first(mixed_ref[0, :, width : 2 * width], pick(m0_ref, seq, slice(width, 2 * width)))
        value = with_first(mixed_ref[0, :, 2 * width :], pick(m0_ref, seq, slice(2 * width, 3 * width)))
        chance_low = p0_ref[0]
        chance = chance_low.astype(F32)
        p_grad = dot_nt(grad, value)
        s_grad = (chance * (p_grad - jnp.sum(p_grad * chance, axis=-1, keepdims=True))).astype(LOW)
        dq = dot(s_grad, key)
        dq = jnp.sum(jnp.where(heads, dq, 0.0), axis=0, keepdims=True) * SCALE
        put(coef_ref, seq, dq, slice(0, width))
        put(coef_ref, seq, query0 * SCALE, slice(width, 2 * width))
        put(coef_ref, seq, own, slice(2 * width, 3 * width))
        inputs = x_ref[0]
        rows_ref[0, 0:1, :] = inputs[0:1, :].astype(F32)
        rows_ref[1] = dot(s_grad, inputs)
        rows_ref[2] = dot(chance_low, inputs)
        firsts, most = groups
        per = width // HD
        for shard, first in enumerate(firsts):
            for turn_of in range(most):
                which, head = divmod(first + turn_of, per)
                head = head if which else 0
                y_ref[shard, 0, turn_of : turn_of + 1, :] = rows_ref[which, head : head + 1, :].astype(LOW)
        from_key = (dot_nt(query, wi_ref[:, width : 2 * width]) * SCALE).astype(LOW)
        from_value = dot_nt(grad, wi_ref[:, 2 * width :]).astype(LOW)
        from_query = dot_nt(jnp.where(heads, dq, 0.0).astype(LOW), wi_ref[:, 0:width])
        from_query = jnp.sum(from_query, axis=0, keepdims=True) + hz_ref[pl.ds(seq, 1), :]
        rows = lax.broadcasted_iota(jnp.int32, (inputs.shape[0], 1), 0)
        back = dot_tn(s_grad, from_key) + dot_tn(chance_low, from_value)
        out_ref[0] = main_ref[0] + back + jnp.where(rows == 0, from_query, 0.0)
        sums_ref[0:1, :] += dq
        held = jnp.sum(chance, axis=-1, keepdims=True)
        sums_ref[1:2, :] += jnp.sum(held * grad.astype(F32), axis=0, keepdims=True)


def last_rows(g0, z0, r2, g2, slope0, wc, we, n0, r1, g1, wo, wi, p0, mixed, m0, x, main, s2, s1, s0, eb, after, shards):
    count, length, wide = mixed.shape
    width = wide // 3
    hidden = slope0.shape[1]
    chunk = 768
    chunks = hidden // chunk
    groups = shard_groups(shards, wide)

    def part(i):
        return jnp.minimum(i, chunks - 1)

    def seq(i):
        return jnp.maximum(i - chunks, 0)

    def per(*shape):
        return pl.BlockSpec((1,) + shape, lambda i: (seq(i),) + (0,) * len(shape))

    row = fixed((1, width))
    rows = fixed((count, width))
    return pl.pallas_call(
        functools.partial(last_kernel, groups=groups),
        grid=(chunks + count,),
        out_shape=(
            jax.ShapeDtypeStruct((count, length, width), F32),
            jax.ShapeDtypeStruct((count, hidden), LOW),
            jax.ShapeDtypeStruct((count, width), LOW),
            jax.ShapeDtypeStruct((count, width), LOW),
            jax.ShapeDtypeStruct((count, wide), F32),
            jax.ShapeDtypeStruct((shards, count, groups[1], width), LOW),
            jax.ShapeDtypeStruct((8, width), F32),
            jax.ShapeDtypeStruct((1, hidden), F32),
        ),
        in_specs=[
            rows, rows, fixed((count, LANES)), row,
            pl.BlockSpec((count, chunk), lambda i: (0, part(i))),
            pl.BlockSpec((chunk, width), lambda i: (part(i), 0)),
            pl.BlockSpec((width, chunk), lambda i: (0, part(i))),
            rows, fixed((count, LANES)), row,
            fixed((width, width)),
            ANYWHERE,
            per(ROW_TILE, length),
            per(length, wide),
            fixed((count, wide)),
            per(length, width),
            per(length, width),
            fixed((8, width)),
            fixed((8, width)),
            fixed((8, width)),
            pl.BlockSpec((1, chunk), lambda i: (0, part(i))),
        ]
        + [ANYWHERE] * len(after),
        out_specs=(
            per(length, width),
            pl.BlockSpec((count, chunk), lambda i: (0, part(i))),
            rows, rows,
            fixed((count, wide)),
            pl.BlockSpec((shards, 1, groups[1], width), lambda i: (0, seq(i), 0, 0)),
            fixed((8, width)),
            pl.BlockSpec((1, chunk), lambda i: (0, part(i))),
        ),
        scratch_shapes=[
            pltpu.VMEM((count, width), F32),
            pltpu.VMEM((count, width), F32),
            pltpu.VMEM((8, width), F32),
            pltpu.VMEM((8, width), F32),
            pltpu.VMEM((3, ROW_TILE, width), F32),
            pltpu.VMEM((width, wide), LOW),
            pltpu.SemaphoreType.DMA,
        ],
        compiler_params=params(60),
        cost_estimate=cost(8 * 1000**3, 36 * MIB),
        name="last_rows",
    )(g0, z0, r2, g2, slope0, wc, we, n0, r1, g1, wo, wi, p0, mixed, m0, x, main, s2, s1, s0, eb, *after)


def flip(value, bit, count):
    return lax.ppermute(value, "rows", [(i, i ^ bit) for i in range(count)])


BITS = ((1, 2), (2, 1))


def first_stage(parts, count):
    return [flip(parts[half], BITS[half][0], count) for half in range(2)]


def second_stage(sends, count):
    return [flip(sends[half], BITS[half][1], count) for half in range(2)]


def sum_low(left_ref, right_ref):
    return (left_ref[...].astype(F32) + right_ref[...].astype(F32)).astype(LOW)


def first_sum_kernel(a0, a1, b0, b1, ga0, ga1, gb0, gb1, *refs):
    sa, sb, ka, kb = refs[-4:]
    sa[...] = sum_low(a0, ga0)
    ka[...] = sum_low(a1, ga1)
    sb[...] = sum_low(b0, gb0)
    kb[...] = sum_low(b1, gb1)


def first_sum(parts, got, after):
    keep0, keep1 = parts[2:]
    rows, width = keep0.shape
    tiles = 4
    block = (rows // 2 // tiles, width)
    top = pl.BlockSpec(block, lambda i: (i, 0))
    bottom = pl.BlockSpec(block, lambda i: (i + tiles, 0))
    result = pl.pallas_call(
        first_sum_kernel,
        grid=(tiles,),
        out_shape=(jax.ShapeDtypeStruct((rows // 2, width), LOW),) * 4,
        in_specs=[top, bottom] * 4 + [ANYWHERE] * len(after),
        out_specs=(top,) * 4,
        compiler_params=params(32),
        cost_estimate=cost(rows * width, 12 * rows * width),
        name="first_sum",
    )(keep0, keep0, keep1, keep1, got[0], got[0], got[1], got[1], *after)
    return result[:2], result[2:]


def second_sum_kernel(a, b, ga, gb, *refs, rest):
    step = pl.program_id(0)
    half = a.shape[1]
    for index, out in enumerate(refs[-rest:]):

        @pl.when(step == index)
        def _():
            out[:, :half] = sum_low(a, ga)
            out[:, half:] = sum_low(b, gb)


def second_sum(keeps, got, count, after):
    rows, width = keeps[0].shape
    rest = count // 4
    block = pl.BlockSpec((rows // rest, width), lambda i: (i, 0))
    shape = (rows // rest, 2 * width)
    return pl.pallas_call(
        functools.partial(second_sum_kernel, rest=rest),
        grid=(rest,),
        out_shape=(jax.ShapeDtypeStruct(shape, LOW),) * rest,
        in_specs=[block] * 4 + [ANYWHERE] * len(after),
        out_specs=(fixed(shape),) * rest,
        compiler_params=params(32),
        cost_estimate=cost(rows * width, 12 * rows * width),
        name="second_sum",
    )(keeps[0], keeps[1], got[0], got[1], *after)


def third_stage(totals, count):
    got = [totals[0]]
    for step in range(1, count // 4):
        pairs = [(i, (i + 4 * step) % count) for i in range(count)]
        got.append(lax.ppermute(totals[step], "rows", pairs))
    return got


def third_sum(got):
    return functools.reduce(lambda left, right: left + right, [part.astype(F32) for part in got])


def places(count):
    me = lax.axis_index("rows")
    tables = []
    for first, second in BITS:
        entries = []
        for one in (first, 0):
            for two in (second, 0):
                for step in range(count // 4):
                    entries.append(((me ^ one ^ two) + 4 * step) % count)
        tables.append(jnp.stack(entries))
    return jnp.stack(tables).astype(jnp.int32)


def whole_grad(parts, count, rows=slice(None)):
    send0, send1, keep0, keep1 = (part[rows] for part in parts)
    full = jnp.concatenate(
        [jnp.concatenate([send0, send1], axis=1), jnp.concatenate([keep0, keep1], axis=1)], axis=0
    )
    return lax.psum_scatter(full.astype(F32), "rows", scatter_dimension=0, tiled=True)


def gather_rows(array, count):
    spread = jnp.broadcast_to(array[None], (count,) + array.shape)
    got = lax.all_to_all(spread, "rows", 0, 0, tiled=True)
    return got.reshape((count * array.shape[0],) + array.shape[1:])


def body(
    token_states, lengths, key_mask, cotangent, attention_in, attention_bias, attention_out, output_bias,
    gain_one, shift_one, expand_weight, expand_bias, contract_weight, contract_bias, gain_two, shift_two,
    projection, passage_table, candidates,
):
    section = lax.axis_index("section")
    is_first = section == 0
    count = lax.axis_size("rows")
    me = lax.axis_index("rows")
    tokens = token_states[0]
    seqs, length, width = tokens.shape
    rows = seqs * length

    bi = attention_bias[0]
    wi, wo, we, wc = attention_in[0], attention_out[0], expand_weight[0], contract_weight[0]
    bo, g1, c1, be, bc, g2, c2 = output_bias, gain_one, shift_one, expand_bias, contract_bias, gain_two, shift_two
    weights = (wi, bi, wo, bo, g1, c1, we, be, wc, bc, g2, c2)
    positions = jnp.arange(length)
    valid = (positions[None, :] < lengths[0][:, None]) & (key_mask[0] == 1) | (positions[None, :] == 0)
    valid = valid.astype(F32)[:, None, :]
    staged = count % 4 == 0 and width // count % ROW_TILE == 0
    cuts = count if staged else 2
    place = places(count) if staged else jnp.asarray([[0, 1], [0, 1]], jnp.int32)

    retrieved = jnp.take(passage_table, candidates, axis=0).astype(F32)
    mixed, x0 = project(token_states, wi, bi)
    message = first_rows(mixed, valid, x0, weights, projection)
    received = lax.ppermute(message, "section", [(0, 1)])
    summary_in, embedding_in = received[:, :width], received[:, width:]
    x0 = x0 + summary_in.astype(F32)
    in_bias = jnp.concatenate([bi[0], jnp.zeros_like(bi[0]), bi[1]])
    mixed0 = (dot(x0.astype(LOW), wi) + in_bias.astype(F32)).astype(LOW).astype(F32)
    chance, context, first, first_low, normal, root, x_low, chance0, early, n0, r1 = attention_forward(
        mixed, mixed0, token_states, x0, valid, wo, bo, g1, c1
    )
    match = jnp.sum(embedding_in.astype(F32)[:, None, :] * retrieved, axis=-1)
    chances = jax.nn.softmax(match, axis=-1)
    weight = TOPK * chances[:, 0]
    scal = jnp.concatenate([jnp.where(is_first, 1.0, weight), jnp.where(is_first, 0.0, 1.0)[None]]).astype(F32)
    first_flat = first_low.reshape(rows, width)
    slope, out, z_grad, feed_grad, sums_two, weight_grads, z0, r2, active0, slope0, *contract = feed_forward(
        place, scal, first_flat, first, we, be, wc, bc, g2, c2, cotangent[0], cuts
    )

    contract_got = first_stage(contract, count) if staged else None
    used_summary = jnp.where(is_first, message[:, :width], summary_in)
    early = jnp.concatenate([active0.astype(LOW), early.astype(LOW), used_summary], axis=1)
    early = gather_rows(early, count)
    expand_sum, h_grad, attended, sums_one, h0, *expand = feed_backward(
        place, feed_grad.reshape(rows, width), slope, wc, we, z_grad, normal, root, g1, first_flat, cuts
    )
    contract_send = ()
    if staged:
        contract_send, contract_keep = first_sum(contract, contract_got, (h0, early))
        contract_got = second_stage(contract_send, count)
        expand_got = first_stage(expand, count)
    mixed_grad, mg0, *rest = attention_backward(
        place, attended, wo, chance, mixed, mixed0, x_low.reshape(rows, width), context.reshape(rows, width),
        tuple(contract_send), cuts,
    )
    after = ()
    if staged:
        contract = second_sum(contract_keep, contract_got, count, (mg0,))
        contract_got = third_stage(contract, count)
        expand_send, expand_keep = first_sum(expand, expand_got, (mg0,))
        expand_got = second_stage(expand_send, count)
        rest_got = first_stage(rest, count)
        after = (contract[0], expand_send[0])
    x_main, sums_in = input_grad(mixed_grad, wi, h_grad, after)

    grad_weight = jnp.sum(weight_grads, axis=1)
    one = jnp.zeros((TOPK,), F32).at[0].set(1.0)
    grad_match = (grad_weight[:, None] * weight[:, None] * (one[None, :] - chances)).astype(LOW)
    embedding_grad = jnp.sum(grad_match.astype(F32)[:, :, None] * retrieved, axis=1).astype(LOW)
    reader_term = (h0 + dot_nt(mg0.astype(LOW), wi)).astype(LOW)
    back = lax.ppermute(jnp.concatenate([reader_term, embedding_grad], axis=1), "section", [(1, 0)])
    embedding_used = jnp.where(is_first, back[:, width:], embedding_grad)
    summary_grad = dot_nt(back[:, width:], projection) + back[:, :width].astype(F32)
    grad_zero = jnp.where(is_first, cotangent[0, :, 0, :].astype(F32) + summary_grad, 0.0)
    x_grad, hidden_zero, feed_zero, attended_zero, coefs, groups, vectors, expand_sum = last_rows(
        grad_zero, z0, r2, g2, slope0, wc, we, n0, r1, g1, wo, wi, chance0, mixed, mixed0, x_low, x_main,
        sums_two, sums_one, sums_in, expand_sum, (), count,
    )

    span = 3 * width // count
    if staged:
        expand = second_sum(expand_keep, expand_got, count, (vectors,))
        rest_send, rest_keep = first_sum(rest, rest_got, (vectors, expand[0]))
        expand_got = third_stage(expand, count)
        rest_got = second_stage(rest_send, count)
        held = (hidden_zero, feed_zero, attended_zero, coefs, groups, vectors, expand_sum, contract_got, rest_send[0])
        held = lax.optimization_barrier(held)
        hidden_zero, feed_zero, attended_zero, coefs, groups, vectors, expand_sum, contract_got, _ = held
        rest = second_sum(rest_keep, rest_got, count, ())
        rest_got = third_stage(rest, count)
        contract = third_sum(contract_got)
        expand = third_sum(expand_got)
        rest = third_sum(rest_got)
        attention_in_grad, attention_out_grad = rest[:span], rest[span:]
    else:
        contract = whole_grad(contract, count)
        expand = whole_grad(expand, count)
        attention_in_grad = whole_grad(rest, count, slice(0, 3 * width // 2))
        attention_out_grad = whole_grad(rest, count, slice(3 * width // 2, None))

    hidden = we.shape[1]
    active_all, first_all = early[:, :hidden], early[:, hidden : hidden + width]
    context_all = early[:, hidden + width : hidden + 2 * width]
    summary_all = early[:, hidden + 2 * width :]

    def shards(array):
        return jnp.swapaxes(array.reshape(array.shape[0], count, -1), 0, 1)

    most = groups.shape[2]
    spread = jnp.broadcast_to(embedding_used[None], (count,) + embedding_used.shape)
    late = jnp.concatenate(
        [
            shards(feed_zero), shards(hidden_zero), shards(attended_zero), shards(coefs.astype(LOW)), spread,
            groups.reshape(count, seqs, -1),
        ],
        axis=2,
    )
    packed = jnp.concatenate([shards(vectors).reshape(count, -1), expand_sum.reshape(count, -1)], axis=1)
    upper = packed.astype(LOW)
    lower = (packed - upper.astype(F32)).astype(LOW)
    packed = jnp.concatenate([upper, lower], axis=1)
    share = packed.shape[1]
    packed = jnp.pad(packed, ((0, 0), (0, late.shape[2] - share)))
    late = lax.all_to_all(jnp.concatenate([late, packed[:, None, :]], axis=1), "rows", 0, 0, tiled=True)
    packed = jnp.sum(late[:, seqs, :share].astype(F32).reshape(count, 2, share // 2), axis=(0, 1))
    late = late[:, :seqs].reshape(count * seqs, -1)
    ends = [width // count, (width + hidden) // count, (2 * width + hidden) // count, (5 * width + hidden) // count]
    ends.append(ends[3] + embedding_used.shape[1])
    contract = contract + dot_tn(late[:, : ends[0]], active_all)
    expand = expand + dot_tn(late[:, ends[0] : ends[1]], first_all)
    attention_out_grad = attention_out_grad + dot_tn(late[:, ends[1] : ends[2]], context_all)
    head = (span * me + jnp.arange(span)) // HD - jnp.asarray(shard_groups(count, 3 * width)[0], jnp.int32)[me]
    for one in range(most):
        part = late[:, ends[2] : ends[3]] * (head == one).astype(LOW)[None]
        attention_in_grad = attention_in_grad + dot_tn(part, late[:, ends[4] + one * width : ends[4] + (one + 1) * width])
    projection_grad = dot_tn(summary_all, late[:, ends[3] : ends[4]])
    part = width // count
    q_bias, v_bias, o_bias, gain1, shift1, c_bias, gain2, shift2 = (packed[i * part : (i + 1) * part] for i in range(8))
    e_bias = packed[8 * part :]
    return (
        out[None],
        x_grad[None],
        attention_in_grad.T[None],
        jnp.stack([q_bias, v_bias])[None],
        attention_out_grad.T[None],
        o_bias[None],
        gain1[None],
        shift1[None],
        expand.T[None],
        e_bias[None],
        contract.T[None],
        c_bias[None],
        gain2[None],
        shift2[None],
        projection_grad,
    )


def solution(mesh):
    in_specs = (
        P("section", "rows", None, None),
        P("section", "rows"),
        P("section", "rows", None),
        P("section", "rows", None, None),
        P("section", None, None),
        P("section", None, None),
        P("section", None, None),
        P("section", None),
        P("section", None),
        P("section", None),
        P("section", None, None),
        P("section", None),
        P("section", None, None),
        P("section", None),
        P("section", None),
        P("section", None),
        P(),
        P(),
        P("rows", None),
    )
    out_specs = (
        P("section", "rows", None, None),
        P("section", "rows", None, None),
        P("section", None, "rows"),
        P("section", None, "rows"),
        P("section", None, "rows"),
        P("section", "rows"),
        P("section", "rows"),
        P("section", "rows"),
        P("section", None, "rows"),
        P("section", "rows"),
        P("section", None, "rows"),
        P("section", "rows"),
        P("section", "rows"),
        P("section", "rows"),
        P(),
    )
    return jax.shard_map(body, mesh=mesh, in_specs=in_specs, out_specs=out_specs, check_vma=False)
```

time: 1560 us -> 360 us (0.23)
  waiting for transfers between devices: 697 us -> 54 us
  matrix products: 393 us -> 13.9 us
  Pallas kernels: 0 us -> 192 us
  local copies, waits for them, and re-layouts: 219 us -> 30.9 us
  other arithmetic: 128 us -> 13.4 us
  blocking collectives: 79.6 us -> 0 us
  starting transfers between devices: 15.3 us -> 46.1 us
  between operations: 18.9 us -> 2.46 us
    reduce_scatter x4 -> x0, waiting for transfers between devices: 641 us -> none  [the longest x1 177 us: body(): lax.psum_scatter(grad_expand_weight, 'rows', scatter_dimension=1, tiled=T...]
    dot_general x71 -> x10, matrix products: 393 us -> 13.9 us  [the longest x7 6.73 us: dot_tn(): return lax.dot_general(left, right, TN, preferred_element_type=F32)]
    pallas_call x0 -> x14, Pallas kernels: none -> 192 us  [the longest x1 42.8 us: attention_backward(): pl.pallas_call(functools.partial(attention_backward_kernel, shards=shards...]
    reshape x18 -> x12, local copies, waits for them, and re-layouts: 101 us -> 2.25 us  [the longest x2 1.28 us: body(): groups.reshape(count, seqs, -1)]
    unnamed x1 -> x0, blocking collectives: 79.6 us -> none
    psum x1 -> x0, waiting for transfers between devices: 52.7 us -> none  [body(): projection_grad = lax.psum(projection_total, 'rows')]
    ppermute x8 -> x23, waiting for transfers between devices: 2.37 us -> 54 us  [the longest x12 27.3 us: flip(): return lax.ppermute(value, 'rows', [(i, i ^ bit) for i in range(count)])]
    convert_element_type x15 -> x0, local copies, waits for them, and re-layouts: 50.7 us -> none  [the longest x6 40.3 us: layer_backward(): jnp.stack([grad_query, grad_key, grad_value], axis=2).astype(jnp.bfloat16)]
  transfers between devices with their start and end apart: 14 -> 25, of which waited for: 6 -> 5; matrix products, arithmetic and copies ran while one was open for 17% -> 6% of each run, Pallas kernels for 0% -> 33%
where the time goes in v1:
time: 360 us; the launch traced here: 353 us
  Pallas kernels  192 us (53%)
  waiting for transfers between devices  54 us (15%)
  starting transfers between devices  46.1 us (13%)
  local copies, waits for them, and re-layouts  30.9 us (9%)
  matrix products  13.9 us (4%)
  other arithmetic  13.4 us (4%)
    pallas_call x1, Pallas kernels, attention_backward(): pl.pallas_call(functools.partial(attention_backward_kernel, shards=shards...  42.8 us
    pallas_call x1, Pallas kernels, feed_forward(): pl.pallas_call(functools.partial(feed_forward_kernel, chunks=chunks, tile...  36.5 us
    pallas_call x1, Pallas kernels, feed_backward(): pl.pallas_call(functools.partial(feed_backward_kernel, chunks=chunks, sha...  32.5 us
    ppermute x12, waiting for transfers between devices, flip(): return lax.ppermute(value, 'rows', [(i, i ^ bit) for i in range(count)])  27.3 us
    ppermute x9, waiting for transfers between devices, third_stage(): got.append(lax.ppermute(totals[step], 'rows', pairs))  26.7 us
    pallas_call x1, Pallas kernels, attention_forward(): pl.pallas_call(attention_forward_kernel, grid=(count,), out_shape=(jax.Sh...  26.7 us
    unnamed x137, local copies, waits for them, and re-layouts  20.9 us
    pallas_call x1, Pallas kernels, last_rows(): pl.pallas_call(functools.partial(last_kernel, groups=groups), grid=(chunk...  17.7 us
  transfers between devices with their start and end apart: 25, of which 5 were waited for; matrix products, arithmetic and copies ran while one was open for 6% of the time, Pallas kernels for 33%

profile of v1, /device:TPU:0, one launch (start us, length us, event | category | flops | bytes accessed | tf_op | source)
XLA Modules:
  0.0 353.1 jit_solution(5431611271551146490)
XLA Ops:
  1.5 2.0 copy-done.2
  4.1 1.5 copy-done.46
  5.7 5.3 %project_qkv.1 = (bf16[4,288,2304]{2,1,0:T(8,128)(2,1)S(1)}, f32[4,768]{1,0:T(4,128)S(1)}) custom-call(bf16[1,4,288,768]{3,2,1,0:T(8,128)(2,1)S(1)} %copy-done.46, bf16[768,2304]{1,0:T(8,128)(2,1)S(1)} %bitcast.101, bf16[2,768]{1,0:T(2,128)(2,1)S(1)} %bitcast.115), custom_call_target="tpu_custom_call" | custom-call | flops 4076863488 | bytes 14680064 | tf_op jit(solution)/shard_map/project_qkv/pallas_call | solution.py:99
  11.3 6.3 %first_rows_forward.1 = bf16[4,896]{1,0:T(4,128)(2,1)S(1)} custom-call(bf16[4,288,2304]{2,1,0:T(8,128)(2,1)S(1)} %get-tuple-element.114.mixed_ref, f32[4,1,288]{2,1,0:T(1,128)S(1)} %fusion.40.valid_ref, f32[4,768]{1,0:T(4,128)S(1)} %get-tuple-element.115.x0_ref, bf16[768,768]{1,0:T(8,128)(2,1)S(1)} %bitcast.114, bf16[1,768]{1,0:T(2,128)(2,1)S(1)} %copy-done.40, ...), custom_call_target="tpu_custom_call" | custom-call | flops 41943040 | bytes 17825792 | tf_op jit(solution)/shard_map/first_rows_forward/pallas_call | solution.py:183
  17.6 2.4 collective-permute-start
  22.6 3.2 fusion.1.m0_ref
  25.8 26.7 %attention_forward.1 = (bf16[4,12,288,288]{3,2,1,0:T(8,128)(2,1)}, bf16[4,288,768]{2,1,0:T(8,128)(2,1)}, f32[4,288,768]{2,1,0:T(8,128)}, bf16[4,288,768]{2,1,0:T...) custom-call(bf16[4,288,2304]{2,1,0:T(8,128)(2,1)} %copy-done.4, ...), custom_call_target="tpu_custom_call" | custom-call | flops 12000000000 | bytes 27262976 | tf_op jit(solution)/shard_map/attention_forward/pallas_call | solution.py:274
  53.1 36.5 %feed_forward.1 = (bf16[1152,3072]{1,0:T(8,128)(2,1)}, f32[4,288,768]{2,1,0:T(8,128)}, f32[4,288,768]{2,1,0:T(8,128)}, bf16[4,288,768]{2,1,0:T(8,128)(2,1)}, f32...) custom-call(s32[2,16]{1,0:T(2,128)} %pad_add_fusion.place_ref, ...), custom_call_target="tpu_custom_call" | custom-call | flops 24999999488 | bytes 52428800 | tf_op jit(solution)/shard_map/feed_forward/pallas_call | solution.py:459
  89.7 2.4 collective-permute-start.1
  92.1 1.5 collective-permute-start.2
  95.5 5.2 %all-to-all-start = ((bf16[16,4,5376]{2,1,0:T(4,128)(2,1)}), bf16[16,4,5376]{2,1,0:T(4,128)(2,1)S(1)}, u32[]{:S(2)}, u32[]{:S(2)}) async-start(bf16[16,4,5376]{2,1,0:T(4,128)(2,1)} %broadcast_in_dim.104), calls=%async_computation | async-start | bytes 1376256 | tf_op jit(solution)/shard_map/all_to_all | solution.py:1056
  100.6 32.5 %feed_backward.1 = (f32[1,3072]{1,0:T(1,128)}, f32[4,288,768]{2,1,0:T(8,128)}, bf16[4,288,768]{2,1,0:T(8,128)(2,1)}, f32[8,768]{1,0:T(8,128)}, f32[4,768]{1,0:T(...) custom-call(s32[2,16]{1,0:T(2,128)} %pad_add_fusion.place_ref, ...), custom_call_target="tpu_custom_call" | custom-call | flops 24999999488 | bytes 52428800 | tf_op jit(solution)/shard_map/feed_backward/pallas_call | solution.py:599
  133.4 2.0 collective-permute-start.6
  135.4 1.4 collective-permute-start.7
  137.4 1.3 copy-done.12
  139.3 3.8 %first_sum.3 = (bf16[192,1536]{1,0:T(8,128)(2,1)}, bf16[192,1536]{1,0:T(8,128)(2,1)}, bf16[192,1536]{1,0:T(8,128)(2,1)S(1)}, bf16[192,1536]{1,0:T(8,128)(2,1)S(1)}) custom-call(bf16[384,1536]{1,0:T(8,128)(2,1)S(1)} %copy-done.11, bf16[384,1536]{1,0:T(8,128)(2,1)S(1)} %copy-done.11, bf16[384,1536]{1,0:T(8,128)(2,1)S(1)} %copy-done.12, ...), custom_call_target="tpu_custom_call" | custom-call | flops 589824 | bytes 7077888 | tf_op jit(solution)/shard_map/first_sum/pallas_call | solution.py:980
  144.6 42.8 %attention_backward.1 = (bf16[4,288,2304]{2,1,0:T(8,128)(2,1)}, f32[4,2304]{1,0:T(4,128)}, bf16[1536,384]{1,0:T(8,128)(2,1)}, bf16[1536,384]{1,0:T(8,128)(2,1)},...) custom-call(s32[2,16]{1,0:T(2,128)} %pad_add_fusion.place_ref, bf16[4,288,768]{2,1,0:T(8,128)(2,1)} %get-tuple-element.125.ag_ref, ...), custom_call_target="tpu_custom_call" | custom-call | flops 24000000000 | bytes 33554432 | tf_op jit(solution)/shard_map/attention_backward/pallas_call | solution.py:709
  187.5 3.2 fusion.4
  190.7 1.3 collective-permute-start.3
  192.9 2.0 collective-permute-start.8
  195.0 3.8 %first_sum.4 = (bf16[768,384]{1,0:T(8,128)(2,1)S(1)}, bf16[768,384]{1,0:T(8,128)(2,1)S(1)}, bf16[768,384]{1,0:T(8,128)(2,1)S(1)}, bf16[768,384]{1,0:T(8,128)(2,1)S(1)}) custom-call(bf16[1536,384]{1,0:T(8,128)(2,1)S(1)} %copy-done.9, bf16[1536,384]{1,0:T(8,128)(2,1)S(1)} %copy-done.9, bf16[1536,384]{1,0:T(8,128)(2,1)S(1)} %copy-done.10, ...), custom_call_target="tpu_custom_call" | custom-call | flops 589824 | bytes 7077888 | tf_op jit(solution)/shard_map/first_sum/pallas_call | solution.py:980
  200.4 1.4 collective-permute-start.10
  203.3 3.1 second_sum.3
  206.4 1.9 collective-permute-start.17
  208.4 6.9 %input_grad.1 = (f32[4,288,768]{2,1,0:T(8,128)S(1)}, f32[8,768]{1,0:T(8,128)S(1)}) custom-call(bf16[4,288,2304]{2,1,0:T(8,128)(2,1)} %get-tuple-element.145.mg_ref, bf16[768,2304]{1,0:T(8,128)(2,1)S(1)} %bitcast.102, f32[4,288,768]{2,1,0:T(8,128)S(1)} %copy-done.52, bf16[48,3072]{1,0:T(8,128)(2,1)S(1)} %get-tuple-element.197.refs_0_, ...), custom_call_target="tpu_custom_call" | custom-call | flops 6000000000 | bytes 16777216 | tf_op jit(solution)/shard_map/input_grad/pallas_call | solution.py:769
  215.3 1.7 copy-done.51
  218.5 2.4 collective-permute-start.18
  220.8 13.5 %collective-permute-done.11.gb = bf16[768,384]{1,0:T(8,128)(2,1)S(1)} collective-permute-done((bf16[768,384]{1,0:T(8,128)(2,1)S(1)}, bf16[768,384]{1,0:T(8,128)(2,1)S(1)}, u32[]{:S(2)}, u32[]{:S(2)}) %collective-permute-start.11) | collective-permute-done | bytes 589856 | tf_op jit(solution)/shard_map/ppermute | solution.py:947
  235.1 3.9 %collective-permute-start.19 = (bf16[48,3072]{1,0:T(8,128)(2,1)S(1)}, bf16[48,3072]{1,0:T(8,128)(2,1)}, u32[]{:S(2)}, u32[]{:S(2)}) collective-permute-start(bf16[48,3072]{1,0:T(8,128)(2,1)S(1)} %get-tuple-element.186), channel_id=1, source_target_pairs={{0,12},{1,13},{2,14},{3,15},{4,0},{5,1},{6,2},{7,3},{8,4},{9,5},{1... | collective-permute-start | bytes 884744 | tf_op jit(solution)/shard_map/ppermute | solution.py:1025
  239.1 17.7 %last_rows.1 = (f32[4,288,768]{2,1,0:T(8,128)}, bf16[4,3072]{1,0:T(4,128)(2,1)}, bf16[4,768]{1,0:T(4,128)(2,1)}, bf16[4,768]{1,0:T(4,128)(2,1)}, f32[4,2304]{1,0...) custom-call(f32[4,768]{1,0:T(4,128)} %fusion.3.g0_ref, ...), custom_call_target="tpu_custom_call" | custom-call | flops 8000000000 | bytes 37748736 | tf_op jit(solution)/shard_map/last_rows/pallas_call | solution.py:890
  260.9 1.3 second_sum.4
  262.3 2.6 first_sum.5
  272.9 4.3 %all-to-all-start.1 = ((bf16[16,5,2864]{2,1,0:T(8,128)(2,1)}), bf16[16,5,2864]{2,1,0:T(8,128)(2,1)}, u32[]{:S(2)}, u32[]{:S(2)}) async-start(bf16[16,5,2864]{2,1,0:T(8,128)(2,1)} %copy.76), calls=%async_computation.1 | async-start | bytes 1507328 | tf_op jit(solution)/shard_map/all_to_all | solution.py:1188
  277.2 1.8 collective-permute-start.12
  279.0 1.5 collective-permute-start.13
  282.4 3.4 collective-permute-start.22
  286.9 13.7 %collective-permute-done.12.ga = bf16[768,384]{1,0:T(8,128)(2,1)S(1)} collective-permute-done((bf16[768,384]{1,0:T(8,128)(2,1)}, bf16[768,384]{1,0:T(8,128)(2,1)S(1)}, u32[]{:S(2)}, u32[]{:S(2)}) %collective-permute-start.12) | collective-permute-done | bytes 589856 | tf_op jit(solution)/shard_map/ppermute | solution.py:947
  300.7 3.0 second_sum.5
  304.4 2.2 collective-permute-start.16
  307.4 1.3 slice.158
  311.8 2.1 add_bitcast_fusion
  315.8 2.0 collective-permute-start.14
  318.9 17.0 %collective-permute-done.21 = bf16[192,768]{1,0:T(8,128)(2,1)} collective-permute-done((bf16[192,768]{1,0:T(8,128)(2,1)}, bf16[192,768]{1,0:T(8,128)(2,1)}, u32[]{:S(2)}, u32[]{:S(2)}) %collective-permute-start.21) | collective-permute-done | bytes 294944 | tf_op jit(solution)/shard_map/ppermute | solution.py:1025
  335.9 2.1 add_bitcast_fusion.1
  338.1 9.6 %collective-permute-done.15 = bf16[192,768]{1,0:T(8,128)(2,1)} collective-permute-done((bf16[192,768]{1,0:T(8,128)(2,1)}, bf16[192,768]{1,0:T(8,128)(2,1)}, u32[]{:S(2)}, u32[]{:S(2)}) %collective-permute-start.15) | collective-permute-done | bytes 294944 | tf_op jit(solution)/shard_map/ppermute | solution.py:1025
  347.7 1.3 convert_add_fusion
  349.0 1.7 fusion.12
  350.7 2.0 fusion.7
  (233 shorter events, 38.2 us)
Async XLA Ops:
  0.6 20.7 %copy-start = (bf16[4096,128]{1,0:T(8,128)(2,1)S(1)}, bf16[4096,128]{1,0:T(8,128)(2,1)}, u32[]{:S(2)}) copy-start(bf16[4096,128]{1,0:T(8,128)(2,1)} %param.39) | copy-start | bytes 3145732
  11.3 8.9 %copy-start.62 = (s32[4,8]{1,0:T(4,128)S(1)}, s32[4,8]{1,0:T(4,128)}, u32[]{:S(2)}) copy-start(s32[4,8]{1,0:T(4,128)} %param.40) | copy-start | bytes 388
  11.3 9.0 %copy-start.39 = (bf16[1,2,768]{2,1,0:T(2,128)(2,1)S(1)}, bf16[1,2,768]{2,1,0:T(2,128)(2,1)}, u32[]{:S(2)}) copy-start(bf16[1,2,768]{2,1,0:T(2,128)(2,1)} %param.27) | copy-start | bytes 9220
  17.6 4.4 %collective-permute-start = (bf16[4,896]{1,0:T(4,128)(2,1)S(1)}, bf16[4,896]{1,0:T(4,128)(2,1)S(1)}, u32[]{:S(2)}, u32[]{:S(2)}) collective-permute-start(bf16[4,896]{1,0:T(4,128)(2,1)S(1)} %first_rows_forward.1), channel_id=1, source_target_pairs={{0,16},{1,17},{2,18},{3,19},{4,20},{5,21},{6,22},{7,23},{8,24},{9,... | collective-permute-start | bytes 21512 | tf_op jit(solution)/shard_map/ppermute | solution.py:1087
  53.1 40.5 %copy-start.59 = (f32[4,1536]{1,0:T(4,128)S(1)}, f32[4,1536]{1,0:T(4,128)}, u32[]{:S(2)}) copy-start(f32[4,1536]{1,0:T(4,128)} %get-tuple-element.134) | copy-start | bytes 73732
  89.7 47.7 %collective-permute-start.1 = (bf16[384,1536]{1,0:T(8,128)(2,1)}, bf16[384,1536]{1,0:T(8,128)(2,1)}, u32[]{:S(2)}, u32[]{:S(2)}) collective-permute-start(bf16[384,1536]{1,0:T(8,128)(2,1)} %get-tuple-element.131), channel_id=1, source_target_pairs={{0,1},{1,0},{2,3},{3,2},{4,5},{5,4},{6,7},{7,6},{8,9},{9,8},{10,11... | collective-permute-start | bytes 3538952 | tf_op jit(solution)/shard_map/ppermute | solution.py:947
  92.1 45.3 %collective-permute-start.2 = (bf16[384,1536]{1,0:T(8,128)(2,1)}, bf16[384,1536]{1,0:T(8,128)(2,1)}, u32[]{:S(2)}, u32[]{:S(2)}) collective-permute-start(bf16[384,1536]{1,0:T(8,128)(2,1)} %get-tuple-element.132), channel_id=1, source_target_pairs={{0,2},{1,3},{2,0},{3,1},{4,6},{5,7},{6,4},{7,5},{8,10},{9,11},{10,... | collective-permute-start | bytes 3538952 | tf_op jit(solution)/shard_map/ppermute | solution.py:947
  95.5 41.7 %all-to-all-start = ((bf16[16,4,5376]{2,1,0:T(4,128)(2,1)}), bf16[16,4,5376]{2,1,0:T(4,128)(2,1)S(1)}, u32[]{:S(2)}, u32[]{:S(2)}) async-start(bf16[16,4,5376]{2,1,0:T(4,128)(2,1)} %broadcast_in_dim.104), calls=%async_computation | async-start | bytes 1376256 | tf_op jit(solution)/shard_map/all_to_all | solution.py:1056
  100.6 32.5 %copy-start.61 = (f32[4,768]{1,0:T(4,128)S(1)}, f32[4,768]{1,0:T(4,128)}, u32[]{:S(2)}) copy-start(f32[4,768]{1,0:T(4,128)} %get-tuple-element.138) | copy-start | bytes 36868
  100.6 36.3 %copy-start.66 = (f32[8]{0:T(128)S(1)}, f32[8]{0:T(128)}, u32[]{:S(2)}) copy-start(f32[8]{0:T(128)} %constant.211.clone.1) | copy-start | bytes 100
  133.4 59.5 %collective-permute-start.6 = (bf16[1536,384]{1,0:T(8,128)(2,1)}, bf16[1536,384]{1,0:T(8,128)(2,1)}, u32[]{:S(2)}, u32[]{:S(2)}) collective-permute-start(bf16[1536,384]{1,0:T(8,128)(2,1)} %get-tuple-element.152), channel_id=1, source_target_pairs={{0,1},{1,0},{2,3},{3,2},{4,5},{5,4},{6,7},{7,6},{8,9},{9,8},{10,11... | collective-permute-start | bytes 3538952 | tf_op jit(solution)/shard_map/ppermute | solution.py:947
  135.4 59.5 %collective-permute-start.7 = (bf16[1536,384]{1,0:T(8,128)(2,1)}, bf16[1536,384]{1,0:T(8,128)(2,1)}, u32[]{:S(2)}, u32[]{:S(2)}) collective-permute-start(bf16[1536,384]{1,0:T(8,128)(2,1)} %get-tuple-element.153), channel_id=1, source_target_pairs={{0,2},{1,3},{2,0},{3,1},{4,6},{5,7},{6,4},{7,5},{8,10},{9,11},{10,... | collective-permute-start | bytes 3538952 | tf_op jit(solution)/shard_map/ppermute | solution.py:947
  144.0 43.5 %copy-start.29 = (bf16[192,1536]{1,0:T(8,128)(2,1)}, bf16[192,1536]{1,0:T(8,128)(2,1)S(1)}, u32[]{:S(2)}) copy-start(bf16[192,1536]{1,0:T(8,128)(2,1)S(1)} %get-tuple-element.148.b) | copy-start | bytes 1769476
  144.0 59.2 %collective-permute-start.4 = (bf16[192,1536]{1,0:T(8,128)(2,1)}, bf16[192,1536]{1,0:T(8,128)(2,1)}, u32[]{:S(2)}, u32[]{:S(2)}) collective-permute-start(bf16[192,1536]{1,0:T(8,128)(2,1)} %get-tuple-element.135.refs_0_), channel_id=1, source_target_pairs={{0,2},{1,3},{2,0},{3,1},{4,6},{5,7},{6,4},{7,5},{8,10},{9,11},{10,... | collective-permute-start | bytes 1769480 | tf_op jit(solution)/shard_map/ppermute | solution.py:947
  144.6 58.7 %collective-permute-start.5 = (bf16[192,1536]{1,0:T(8,128)(2,1)}, bf16[192,1536]{1,0:T(8,128)(2,1)}, u32[]{:S(2)}, u32[]{:S(2)}) collective-permute-start(bf16[192,1536]{1,0:T(8,128)(2,1)} %get-tuple-element.136.refs_1_), channel_id=1, source_target_pairs={{0,1},{1,0},{2,3},{3,2},{4,5},{5,4},{6,7},{7,6},{8,9},{9,8},{10,11... | collective-permute-start | bytes 1769480 | tf_op jit(solution)/shard_map/ppermute | solution.py:947
  187.5 7.4 %copy-start.9 = (bf16[1536,384]{1,0:T(8,128)(2,1)S(1)}, bf16[1536,384]{1,0:T(8,128)(2,1)}, u32[]{:S(2)}) copy-start(bf16[1536,384]{1,0:T(8,128)(2,1)} %get-tuple-element.150.a0.a1) | copy-start | bytes 3538948
  187.5 7.4 %copy-start.10 = (bf16[1536,384]{1,0:T(8,128)(2,1)S(1)}, bf16[1536,384]{1,0:T(8,128)(2,1)}, u32[]{:S(2)}) copy-start(bf16[1536,384]{1,0:T(8,128)(2,1)} %get-tuple-element.151.b0.b1) | copy-start | bytes 3538948
  187.5 7.4 %copy-start.31 = (f32[4,2304]{1,0:T(4,128)S(1)}, f32[4,2304]{1,0:T(4,128)}, u32[]{:S(2)}) copy-start(f32[4,2304]{1,0:T(4,128)} %get-tuple-element.137.refs_0_) | copy-start | bytes 110596
  190.7 11.1 %collective-permute-start.3 = (bf16[4,896]{1,0:T(4,128)(2,1)S(1)}, bf16[4,896]{1,0:T(4,128)(2,1)S(1)}, u32[]{:S(2)}, u32[]{:S(2)}) collective-permute-start(bf16[4,896]{1,0:T(4,128)(2,1)S(1)} %pad_maximum_fusion.2), channel_id=1, source_target_pairs={{16,0},{17,1},{18,2},{19,3},{20,4},{21,5},{22,6},{23,7},{24,8},{25... | collective-permute-start | bytes 21512 | tf_op jit(solution)/shard_map/ppermute | solution.py:1135
  192.9 69.4 %collective-permute-start.8 = (bf16[1536,384]{1,0:T(8,128)(2,1)}, bf16[1536,384]{1,0:T(8,128)(2,1)S(1)}, u32[]{:S(2)}, u32[]{:S(2)}) collective-permute-start(bf16[1536,384]{1,0:T(8,128)(2,1)} %get-tuple-element.163), channel_id=1, source_target_pairs={{0,1},{1,0},{2,3},{3,2},{4,5},{5,4},{6,7},{7,6},{8,9},{9,8},{10,11... | collective-permute-start | bytes 3538952 | tf_op jit(solution)/shard_map/ppermute | solution.py:947
  194.9 8.4 %copy-start.28 = (bf16[192,1536]{1,0:T(8,128)(2,1)S(1)}, bf16[192,1536]{1,0:T(8,128)(2,1)}, u32[]{:S(2)}) copy-start(bf16[192,1536]{1,0:T(8,128)(2,1)} %copy-done.27) | copy-start | bytes 1769476
  194.9 8.4 %copy-start.30 = (bf16[192,1536]{1,0:T(8,128)(2,1)S(1)}, bf16[192,1536]{1,0:T(8,128)(2,1)}, u32[]{:S(2)}) copy-start(bf16[192,1536]{1,0:T(8,128)(2,1)} %copy-done.29) | copy-start | bytes 1769476
  194.9 13.4 %copy-start.3 = (bf16[1,768,2304]{2,1,0:T(8,128)(2,1)S(1)}, bf16[1,768,2304]{2,1,0:T(8,128)(2,1)}, u32[]{:S(2)}) copy-start(bf16[1,768,2304]{2,1,0:T(8,128)(2,1)} %param.26) | copy-start | bytes 10616836
  194.9 13.4 %copy-start.52 = (f32[4,288,768]{2,1,0:T(8,128)S(1)}, f32[4,288,768]{2,1,0:T(8,128)}, u32[]{:S(2)}) copy-start(f32[4,288,768]{2,1,0:T(8,128)} %get-tuple-element.146.hgrad_ref) | copy-start | bytes 10616836
  200.4 17.3 %collective-permute-start.10 = (bf16[768,384]{1,0:T(8,128)(2,1)S(1)}, bf16[768,384]{1,0:T(8,128)(2,1)S(1)}, u32[]{:S(2)}, u32[]{:S(2)}) collective-permute-start(bf16[768,384]{1,0:T(8,128)(2,1)S(1)} %get-tuple-element.154.refs_1_), channel_id=1, source_target_pairs={{0,2},{1,3},{2,0},{3,1},{4,6},{5,7},{6,4},{7,5},{8,10},{9,11},{10,... | collective-permute-start | bytes 1769480 | tf_op jit(solution)/shard_map/ppermute | solution.py:947
  201.8 32.5 %collective-permute-start.11 = (bf16[768,384]{1,0:T(8,128)(2,1)S(1)}, bf16[768,384]{1,0:T(8,128)(2,1)S(1)}, u32[]{:S(2)}, u32[]{:S(2)}) collective-permute-start(bf16[768,384]{1,0:T(8,128)(2,1)S(1)} %get-tuple-element.168), channel_id=1, source_target_pairs={{0,1},{1,0},{2,3},{3,2},{4,5},{5,4},{6,7},{7,6},{8,9},{9,8},{10,11... | collective-permute-start | bytes 1769480 | tf_op jit(solution)/shard_map/ppermute | solution.py:947
  203.2 59.1 %collective-permute-start.9 = (bf16[1536,384]{1,0:T(8,128)(2,1)}, bf16[1536,384]{1,0:T(8,128)(2,1)}, u32[]{:S(2)}, u32[]{:S(2)}) collective-permute-start(bf16[1536,384]{1,0:T(8,128)(2,1)} %get-tuple-element.164), channel_id=1, source_target_pairs={{0,2},{1,3},{2,0},{3,1},{4,6},{5,7},{6,4},{7,5},{8,10},{9,11},{10,... | collective-permute-start | bytes 3538952 | tf_op jit(solution)/shard_map/ppermute | solution.py:947
  206.4 61.7 %collective-permute-start.17 = (bf16[48,3072]{1,0:T(8,128)(2,1)}, bf16[48,3072]{1,0:T(8,128)(2,1)}, u32[]{:S(2)}, u32[]{:S(2)}) collective-permute-start(bf16[48,3072]{1,0:T(8,128)(2,1)} %get-tuple-element.184), channel_id=1, source_target_pairs={{0,4},{1,5},{2,6},{3,7},{4,8},{5,9},{6,10},{7,11},{8,12},{9,13},{1... | collective-permute-start | bytes 884744 | tf_op jit(solution)/shard_map/ppermute | solution.py:1025
  218.5 49.7 %collective-permute-start.18 = (bf16[48,3072]{1,0:T(8,128)(2,1)S(1)}, bf16[48,3072]{1,0:T(8,128)(2,1)}, u32[]{:S(2)}, u32[]{:S(2)}) collective-permute-start(bf16[48,3072]{1,0:T(8,128)(2,1)S(1)} %get-tuple-element.185), channel_id=1, source_target_pairs={{0,8},{1,9},{2,10},{3,11},{4,12},{5,13},{6,14},{7,15},{8,0},{9,1},... | collective-permute-start | bytes 884744 | tf_op jit(solution)/shard_map/ppermute | solution.py:1025
  235.1 33.0 %collective-permute-start.19 = (bf16[48,3072]{1,0:T(8,128)(2,1)S(1)}, bf16[48,3072]{1,0:T(8,128)(2,1)}, u32[]{:S(2)}, u32[]{:S(2)}) collective-permute-start(bf16[48,3072]{1,0:T(8,128)(2,1)S(1)} %get-tuple-element.186), channel_id=1, source_target_pairs={{0,12},{1,13},{2,14},{3,15},{4,0},{5,1},{6,2},{7,3},{8,4},{9,5},{1... | collective-permute-start | bytes 884744 | tf_op jit(solution)/shard_map/ppermute | solution.py:1025
  239.1 17.8 %copy-start.20 = (bf16[768,384]{1,0:T(8,128)(2,1)S(1)}, bf16[768,384]{1,0:T(8,128)(2,1)}, u32[]{:S(2)}) copy-start(bf16[768,384]{1,0:T(8,128)(2,1)} %copy-done.19) | copy-start | bytes 1769476
  262.3 7.5 %copy-start.58 = (bf16[4,3072]{1,0:T(4,128)(2,1)S(1)}, bf16[4,3072]{1,0:T(4,128)(2,1)}, u32[]{:S(2)}) copy-start(bf16[4,3072]{1,0:T(4,128)(2,1)} %get-tuple-element.188) | copy-start | bytes 73732
  262.3 7.6 %copy-start.63 = (bf16[4,768]{1,0:T(4,128)(2,1)S(1)}, bf16[4,768]{1,0:T(4,128)(2,1)}, u32[]{:S(2)}) copy-start(bf16[4,768]{1,0:T(4,128)(2,1)} %get-tuple-element.189) | copy-start | bytes 18436
  262.3 7.7 %copy-start.57 = (f32[4,2304]{1,0:T(4,128)S(1)}, f32[4,2304]{1,0:T(4,128)}, u32[]{:S(2)}) copy-start(f32[4,2304]{1,0:T(4,128)} %get-tuple-element.190) | copy-start | bytes 110596
  271.8 8.6 %copy-start.67 = (s32[16]{0:T(128)S(1)}, s32[16]{0:T(128)}, u32[]{:S(2)}) copy-start(s32[16]{0:T(128)} %constant.216.clone) | copy-start | bytes 196
  271.9 28.8 %copy-start.16 = (bf16[768,384]{1,0:T(8,128)(2,1)S(1)}, bf16[768,384]{1,0:T(8,128)(2,1)}, u32[]{:S(2)}) copy-start(bf16[768,384]{1,0:T(8,128)(2,1)} %copy-done.15) | copy-start | bytes 1769476
  271.9 28.8 %copy-start.18 = (bf16[768,384]{1,0:T(8,128)(2,1)S(1)}, bf16[768,384]{1,0:T(8,128)(2,1)}, u32[]{:S(2)}) copy-start(bf16[768,384]{1,0:T(8,128)(2,1)} %copy-done.17) | copy-start | bytes 1769476
  272.9 34.4 %all-to-all-start.1 = ((bf16[16,5,2864]{2,1,0:T(8,128)(2,1)}), bf16[16,5,2864]{2,1,0:T(8,128)(2,1)}, u32[]{:S(2)}, u32[]{:S(2)}) async-start(bf16[16,5,2864]{2,1,0:T(8,128)(2,1)} %copy.76), calls=%async_computation.1 | async-start | bytes 1507328 | tf_op jit(solution)/shard_map/all_to_all | solution.py:1188
  277.2 23.3 %collective-permute-start.12 = (bf16[768,384]{1,0:T(8,128)(2,1)}, bf16[768,384]{1,0:T(8,128)(2,1)S(1)}, u32[]{:S(2)}, u32[]{:S(2)}) collective-permute-start(bf16[768,384]{1,0:T(8,128)(2,1)} %copy-done.48), channel_id=1, source_target_pairs={{0,2},{1,3},{2,0},{3,1},{4,6},{5,7},{6,4},{7,5},{8,10},{9,11},{10,... | collective-permute-start | bytes 1769480 | tf_op jit(solution)/shard_map/ppermute | solution.py:947
  279.0 21.7 %collective-permute-start.13 = (bf16[768,384]{1,0:T(8,128)(2,1)}, bf16[768,384]{1,0:T(8,128)(2,1)}, u32[]{:S(2)}, u32[]{:S(2)}) collective-permute-start(bf16[768,384]{1,0:T(8,128)(2,1)} %copy-done.47), channel_id=1, source_target_pairs={{0,1},{1,0},{2,3},{3,2},{4,5},{5,4},{6,7},{7,6},{8,9},{9,8},{10,11... | collective-permute-start | bytes 1769480 | tf_op jit(solution)/shard_map/ppermute | solution.py:947
  282.4 33.4 %collective-permute-start.22 = (bf16[192,768]{1,0:T(8,128)(2,1)}, bf16[192,768]{1,0:T(8,128)(2,1)}, u32[]{:S(2)}, u32[]{:S(2)}) collective-permute-start(bf16[192,768]{1,0:T(8,128)(2,1)} %get-tuple-element.196), channel_id=1, source_target_pairs={{0,12},{1,13},{2,14},{3,15},{4,0},{5,1},{6,2},{7,3},{8,4},{9,5},{1... | collective-permute-start | bytes 884744 | tf_op jit(solution)/shard_map/ppermute | solution.py:1025
  285.8 50.1 %collective-permute-start.21 = (bf16[192,768]{1,0:T(8,128)(2,1)}, bf16[192,768]{1,0:T(8,128)(2,1)}, u32[]{:S(2)}, u32[]{:S(2)}) collective-permute-start(bf16[192,768]{1,0:T(8,128)(2,1)} %get-tuple-element.195), channel_id=1, source_target_pairs={{0,8},{1,9},{2,10},{3,11},{4,12},{5,13},{6,14},{7,15},{8,0},{9,1},... | collective-permute-start | bytes 884744 | tf_op jit(solution)/shard_map/ppermute | solution.py:1025
  285.8 50.1 %collective-permute-start.20 = (bf16[192,768]{1,0:T(8,128)(2,1)}, bf16[192,768]{1,0:T(8,128)(2,1)}, u32[]{:S(2)}, u32[]{:S(2)}) collective-permute-start(bf16[192,768]{1,0:T(8,128)(2,1)} %get-tuple-element.194), channel_id=1, source_target_pairs={{0,4},{1,5},{2,6},{3,7},{4,8},{5,9},{6,10},{7,11},{8,12},{9,13},{1... | collective-permute-start | bytes 884744 | tf_op jit(solution)/shard_map/ppermute | solution.py:1025
  304.4 33.7 %collective-permute-start.16 = (bf16[192,768]{1,0:T(8,128)(2,1)}, bf16[192,768]{1,0:T(8,128)(2,1)}, u32[]{:S(2)}, u32[]{:S(2)}) collective-permute-start(bf16[192,768]{1,0:T(8,128)(2,1)} %get-tuple-element.177), channel_id=1, source_target_pairs={{0,12},{1,13},{2,14},{3,15},{4,0},{5,1},{6,2},{7,3},{8,4},{9,5},{1... | collective-permute-start | bytes 884744 | tf_op jit(solution)/shard_map/ppermute | solution.py:1025
  306.6 41.0 %collective-permute-start.15 = (bf16[192,768]{1,0:T(8,128)(2,1)}, bf16[192,768]{1,0:T(8,128)(2,1)}, u32[]{:S(2)}, u32[]{:S(2)}) collective-permute-start(bf16[192,768]{1,0:T(8,128)(2,1)} %get-tuple-element.176), channel_id=1, source_target_pairs={{0,8},{1,9},{2,10},{3,11},{4,12},{5,13},{6,14},{7,15},{8,0},{9,1},... | collective-permute-start | bytes 884744 | tf_op jit(solution)/shard_map/ppermute | solution.py:1025
  314.0 33.7 %copy-start.33 = (bf16[192,768]{1,0:T(8,128)(2,1)S(1)}, bf16[192,768]{1,0:T(8,128)(2,1)}, u32[]{:S(2)}) copy-start(bf16[192,768]{1,0:T(8,128)(2,1)} %copy-done.32) | copy-start | bytes 884740
  315.8 31.9 %collective-permute-start.14 = (bf16[192,768]{1,0:T(8,128)(2,1)S(1)}, bf16[192,768]{1,0:T(8,128)(2,1)S(1)}, u32[]{:S(2)}, u32[]{:S(2)}) collective-permute-start(bf16[192,768]{1,0:T(8,128)(2,1)S(1)} %copy-done.50), channel_id=1, source_target_pairs={{0,4},{1,5},{2,6},{3,7},{4,8},{5,9},{6,10},{7,11},{8,12},{9,13},{1... | collective-permute-start | bytes 884744 | tf_op jit(solution)/shard_map/ppermute | solution.py:1025
  318.9 31.8 %copy-start.55 = (f32[144,768]{1,0:T(8,128)S(1)}, f32[144,768]{1,0:T(8,128)}, u32[]{:S(2)}) copy-start(f32[144,768]{1,0:T(8,128)} %fusion.27) | copy-start | bytes 1327108
  (45 other events, 154.0 us)
